TPU v7x, 32 devices: a whole 2x2x4 slice. The times are simulated.
32 devices in a mesh: aux: 16 (over z, x, core), pair: 2 (over y).
Axes of the slice: x: 2, y: 2, z: 4, core: 2. Of those that a mesh axis runs over, the one named last changes fastest.
Arguments:
- three_index: bfloat16 [14336, 512], P('aux', 'pair'), may hold values from -0.375 to 0.375
- occupied_energy: float32 [64], replicated, may hold values from -2 to -0.3
- virtual_energy: float32 [20096], replicated, may hold values from 0.5 to 4
- tile_occupied: int32 [4], replicated, may hold values from 0 to 63
- tile_virtual: int32 [4], replicated, may hold values from 0 to 156
- tile_exponent: int32 [4], replicated, may hold values from -1 to 1
Outputs:
- gamma_terms: bfloat16 [14336, 512], P('aux', 'pair')
All inputs are finite; a program needn't handle non-finite values.
Results may differ from a plain program's by a relative error of at most 0.0048.
Values may be sent and summed in bfloat16 or wider, within the bound.
A program may use at most 64 MiB of HBM per device.

v0:
```python
import jax
import jax.numpy as jnp
from jax import lax
from jax.sharding import PartitionSpec as P

TS = 128
VT = 157


def column_scale(tile_exponent):
    factor = jnp.where(tile_exponent == -1, 0.5, jnp.where(tile_exponent == 1, 2.0, 1.0)).astype(
        jnp.float32
    )
    return jnp.repeat(factor, TS)


def column_energy(occupied_energy, virtual_energy, tile_occupied, tile_virtual):
    virtual_cols = virtual_energy.reshape(VT, TS)[tile_virtual].reshape(-1)
    occupied_cols = jnp.repeat(occupied_energy[tile_occupied], TS)
    return virtual_cols - occupied_cols


def make_amplitude(coulomb, row_energy, row_scale, own_energy, own_scale):
    return (
        coulomb
        * (row_scale * row_scale)[:, None]
        * own_scale[None, :]
        / (row_energy[:, None] + own_energy[None, :])
    ).astype(jnp.bfloat16)


def body(three_index, occupied_energy, virtual_energy, tile_occupied, tile_virtual, tile_exponent):
    width_local = three_index.shape[1]
    col_scale = column_scale(tile_exponent)
    col_energy = column_energy(occupied_energy, virtual_energy, tile_occupied, tile_virtual)
    offset = lax.axis_index("pair") * width_local
    own_energy = lax.dynamic_slice_in_dim(col_energy, offset, width_local)
    own_scale = lax.dynamic_slice_in_dim(col_scale, offset, width_local)
    contract = (((0,), (0,)), ((), ()))
    gathered = lax.all_gather(three_index, "pair", axis=1, tiled=True)
    coulomb = lax.dot_general(gathered, three_index, contract, preferred_element_type=jnp.float32)
    summed = lax.psum(coulomb, "aux")
    amplitude = make_amplitude(summed, col_energy, col_scale, own_energy, own_scale)
    result = jnp.dot(gathered, amplitude, preferred_element_type=jnp.float32)
    return result.astype(jnp.bfloat16)


def solution(mesh):
    placed = (P("aux", "pair"), P(), P(), P(), P(), P())
    return jax.shard_map(
        body, mesh=mesh, in_specs=placed, out_specs=P("aux", "pair"), check_vma=False
    )
```

profile of v0, /device:TPU:0, one launch (start us, length us, event | category | flops | bytes accessed | tf_op | source)
XLA Modules:
  0.0 123.7 jit_solution(7261876918825973244)
XLA Ops:
  6.5 0.0 copy-start
  6.5 0.0 copy-start.2
  6.5 0.0 all-reduce.2.cloned.1.call-start
  6.5 14.5 %all_gather.3 = bf16[896,512]{1,0:T(8,128)(2,1)S(1)} all-gather(bf16[896,256]{1,0:T(8,128)(2,1)} %param.6), channel_id=1, replica_groups=mesh['aux'=16,'pair'=2] {'pair'}, dimensions={1}, use_global_device_ids=true | all-gather | bytes 1376256 | tf_op jit(solution)/shard_map/all_gather | solution.py:40
  21.1 0.0 copy-done.2
  21.1 1.3 %fusion.5 = f32[512,256]{1,0:T(8,128)} fusion(bf16[896,512]{1,0:T(8,128)(2,1)S(1)} %all_gather.3, bf16[896,256]{1,0:T(8,128)(2,1)S(1)} %copy-done.2), kind=kOutput, calls=%fused_computation.18 | convolution fusion | flops 234881024 | bytes 1900544 | tf_op jit(solution)/shard_map/dot_general | solution.py:41
  22.4 0.0 copy-start.3
  22.4 0.0 copy-start.1
  22.4 0.0 all-reduce.2.cloned.1.call-update
  22.4 0.6 copy-done.3
  23.0 0.6 copy-done.4
  23.7 0.6 copy-done.5
  24.3 0.0 copy-done
  24.3 0.6 gather_fusion
  24.9 0.0 copy-done.1
  24.9 0.6 gather_fusion.1
  25.5 0.1 subtract_bitcast_fusion
  25.6 0.1 broadcast_bitcast_fusion
  25.7 0.1 dynamic_slice.7
  25.8 0.1 dynamic_slice.6
  25.8 0.1 bitcast_multiply_fusion
  25.9 88.2 %all-reduce.2.cloned.1.call-done = f32[512,256]{1,0:T(8,128)} async-done(((f32[512,256]{1,0:T(8,128)}), f32[512,256]{1,0:T(8,128)}) %all-reduce.2.cloned.1.call-update) | async-done | bytes 524304 | tf_op jit(solution)/shard_map/psum | solution.py:42
  114.1 1.7 %fusion = bf16[896,256]{0,1:T(8,128)(2,1)S(1)} fusion(bf16[896,512]{1,0:T(8,128)(2,1)S(1)} %all_gather.3, f32[512,256]{1,0:T(8,128)} %all-reduce.2.cloned.1.call-done, f32[256]{0:T(256)S(1)} %dynamic_slice.7, f32[512]{0:T(512)S(1)} %subtract_bitcast_fusion, f32[256]{0:T(256)S(1)} %dynamic_slice.6, f32[512]{0:T(512)S(1)} %bitcast_multiply_fusion), kind=kOutput, calls=%fused_computation.3 | convolution fusion | flops 235765760 | bytes 1906688 | tf_op jit(solution)/shard_map/dot_general | solution.py:44
  115.8 1.0 copy.8
  (7 shorter events, 0.0 us)
Async XLA Ops:
  6.5 17.8 %copy-start = (f32[20096]{0:T(1024)S(1)}, f32[20096]{0:T(1024)}, u32[]{:S(2)}) copy-start(f32[20096]{0:T(1024)} %param.8) | copy-start | bytes 241156
  6.5 14.5 %copy-start.2 = (bf16[896,256]{1,0:T(8,128)(2,1)S(1)}, bf16[896,256]{1,0:T(8,128)(2,1)}, u32[]{:S(2)}) copy-start(bf16[896,256]{1,0:T(8,128)(2,1)} %param.6) | copy-start | bytes 1376260
  6.5 107.5 %all-reduce.2.cloned.1.call-start = ((), (), s32[]{:S(2)}) async-start(), calls=%async_computation | async-start | bytes 1048576 | tf_op jit(solution)/shard_map/psum | solution.py:42
  22.4 0.7 copy-start.3
  22.4 2.5 %copy-start.1 = (f32[64]{0:T(128)S(1)}, f32[64]{0:T(128)}, u32[]{:S(2)}) copy-start(f32[64]{0:T(128)} %param.7) | copy-start | bytes 772
  23.0 0.7 copy-start.4
  23.7 0.7 copy-start.5
Sparse Core Ops, SparseCore 0:
  22.5 91.5 all-reduce.1
where the time goes:
time: 124 us
  waiting for transfers between devices  88.2 us (71%)
  blocking collectives  14.5 us (12%)
  between operations  13.4 us (11%)
  local copies, waits for them, and re-layouts  4.34 us (4%)
  matrix products  3 us (2%)
    psum x1, waiting for transfers between devices, body(): summed = lax.psum(coulomb, 'aux')  88.2 us
    all_gather x1, blocking collectives, body(): gathered = lax.all_gather(three_index, 'pair', axis=1, tiled=True)  14.5 us
  transfers between devices with their start and end apart: 1, of which 1 were waited for; matrix products, arithmetic and copies ran while one was open for 1% of the time, Pallas kernels for 0%

commit v1 on v0

--- a/solution.py
+++ b/solution.py
@@ -1,10 +1,17 @@
+import functools
+
 import jax
 import jax.numpy as jnp
 from jax import lax
+from jax.experimental import pallas as pl
+from jax.experimental.pallas import tpu as pltpu
 from jax.sharding import PartitionSpec as P
 
 TS = 128
 VT = 157
+F32 = jnp.float32
+BF16 = jnp.bfloat16
+MESH = pl.DeviceIdType.MESH
 
 
 def column_scale(tile_exponent):
@@ -29,7 +36,9 @@
     ).astype(jnp.bfloat16)
 
 
-def body(three_index, occupied_energy, virtual_energy, tile_occupied, tile_virtual, tile_exponent):
+def general_body(
+    three_index, occupied_energy, virtual_energy, tile_occupied, tile_virtual, tile_exponent
+):
     width_local = three_index.shape[1]
     col_scale = column_scale(tile_exponent)
     col_energy = column_energy(occupied_energy, virtual_energy, tile_occupied, tile_virtual)
@@ -45,8 +54,290 @@
     return result.astype(jnp.bfloat16)
 
 
+def tn_dot(a, b):
+    return lax.dot_general(a, b, (((0,), (0,)), ((), ())), preferred_element_type=F32)
+
+
+def nt_dot(a, b):
+    return lax.dot_general(a, b, (((1,), (1,)), ((), ())), preferred_element_type=F32)
+
+
+def nn_dot(a, b):
+    return jnp.dot(a, b, preferred_element_type=F32)
+
+
+def kernel(
+    Q, b_ref, ve_ref, occ_ref, to_ref, tv_ref, te_ref, out_ref,
+    other, own_c, off_c, own_core, off_core, own_part, off_part, own_got, off_got,
+    own_amp, off_amp, stage, energy,
+    b_s, b_r, core_s, core_r, own_s, own_r, off_s, off_r, owna_s, owna_r, offa_s, offa_r, fw_s, fw_r,
+):
+    rows = b_ref.shape[0]
+    half = rows // 2
+    piece = TS // Q
+    aux = lax.axis_index("aux")
+    j = lax.axis_index("pair")
+    core = lax.rem(aux, 2)
+    q = lax.div(aux, 2)
+    G = 2 * Q
+    g = j * Q + q
+
+    def dev(chip, which):
+        return {"aux": 2 * lax.rem(chip, Q) + which, "pair": lax.div(chip, Q)}
+
+    def remote(src, dst, send, recv, target):
+        return pltpu.make_async_remote_copy(
+            src_ref=src, dst_ref=dst, send_sem=send, recv_sem=recv,
+            device_id=target, device_id_type=MESH,
+        )
+
+    def others(n, me, f):
+        def step(i, carry):
+            f(lax.rem(me + i, n))
+            return carry
+        lax.fori_loop(1, n, step, 0)
+
+    sibling = dev(g, 1 - core)
+    across = dev(lax.rem(g + Q, G), core)
+
+    barrier = pltpu.get_barrier_semaphore()
+    pl.semaphore_signal(barrier, inc=1, device_id=sibling, device_id_type=MESH)
+    others(G, g, lambda t: pl.semaphore_signal(
+        barrier, inc=1, device_id=dev(t, core), device_id_type=MESH))
+
+    for t in range(4):
+        energy[t:t + 1, :] = ve_ref[pl.ds(tv_ref[t], 1), :] - occ_ref[to_ref[t]]
+    own_c[...] = tn_dot(b_ref[...], b_ref[...])
+    pl.semaphore_wait(barrier, G)
+
+    mine = pl.multiple_of(core * TS, TS)
+    theirs = pl.multiple_of((1 - core) * TS, TS)
+    at_q = pl.multiple_of(q * piece, piece)
+
+    def send_b(k):
+        first = pl.multiple_of((j if k == 0 else 1 - j) * half, half)
+        return remote(b_ref.at[pl.ds(first, half)], other.at[pl.ds(first, half)],
+                      b_s.at[k], b_r.at[k], across)
+
+    def got_b(k):
+        first = pl.multiple_of((1 - j if k == 0 else j) * half, half)
+        return remote(b_ref.at[pl.ds(first, half)], other.at[pl.ds(first, half)],
+                      b_s.at[k], b_r.at[k], across)
+
+    def core_copy(k, src, dst):
+        return remote(src.at[pl.ds(theirs, TS)], dst, core_s.at[k], core_r.at[k], sibling)
+
+    send_b(0).start()
+    core_copy(0, own_c, own_core).start()
+    core_copy(0, own_c, own_core).wait_recv()
+    own_core[...] += own_c[pl.ds(mine, TS), :]
+    own_part[...] = own_core[...].astype(BF16)
+
+    def own_scatter(t):
+        return remote(own_part.at[pl.ds(pl.multiple_of(t * piece, piece), piece)], own_got.at[q],
+                      own_s.at[t], own_r.at[q], dev(j * Q + t, core))
+
+    def own_arrival(p):
+        return remote(own_part.at[pl.ds(0, piece)], own_got.at[p],
+                      own_s.at[p], own_r.at[p], dev(j * Q + p, core))
+
+    others(Q, q, lambda t: own_scatter(t).start())
+
+    got_b(0).wait_recv()
+    send_b(0).wait_send()
+    send_b(1).start()
+    here = pl.multiple_of((1 - j) * half, half)
+
+    @pl.when(j == 0)
+    def _():
+        off_c[...] = tn_dot(b_ref[pl.ds(here, half), :], other[pl.ds(here, half), :])
+
+    @pl.when(j == 1)
+    def _():
+        off_c[...] = tn_dot(other[pl.ds(here, half), :], b_ref[pl.ds(here, half), :])
+
+    core_copy(1, off_c, off_core).start()
+
+    def scale(t):
+        e = te_ref[t]
+        return jnp.where(e == -1, 0.5, jnp.where(e == 1, 2.0, 1.0)).astype(F32)
+
+    def down(row):
+        shape = (piece, TS)
+        pick = lax.broadcasted_iota(jnp.int32, shape, 1) == (
+            lax.broadcasted_iota(jnp.int32, shape, 0) + q * piece)
+        return jnp.sum(jnp.where(pick, row, 0.0), axis=1, keepdims=True)
+
+    def add_own(i, total):
+        p = lax.rem(q + i, Q)
+        own_arrival(p).wait_recv()
+        return total + own_got[p].astype(F32)
+
+    own_total = lax.fori_loop(1, Q, add_own, own_core[pl.ds(at_q, piece), :])
+    own_rows = pl.ds(pl.multiple_of(core * TS + q * piece, piece), piece)
+    row_e = down(energy[pl.ds(2 * j + core, 1), :])
+    row_s = scale(2 * j + core)
+    for h in range(2):
+        col_e = energy[pl.ds(2 * j + h, 1), :]
+        col_s = scale(2 * j + h)
+        own_amp[own_rows, h * TS:(h + 1) * TS] = (
+            own_total[:, h * TS:(h + 1) * TS] * (row_s * row_s) * col_s / (row_e + col_e)
+        ).astype(BF16)
+
+    def own_gather(t):
+        return remote(own_amp.at[own_rows], own_amp.at[own_rows],
+                      owna_s.at[t], owna_r.at[q], dev(j * Q + t, core))
+
+    def own_gathered(p):
+        place = own_amp.at[pl.ds(pl.multiple_of(core * TS + p * piece, piece), piece)]
+        return remote(place, place, owna_s.at[p], owna_r.at[p], dev(j * Q + p, core))
+
+    others(Q, q, lambda t: own_gather(t).start())
+
+    core_copy(1, off_c, off_core).wait_recv()
+    off_core[...] += off_c[pl.ds(mine, TS), :]
+    for h in range(2):
+        off_part[h] = off_core[:, h * TS:(h + 1) * TS].astype(BF16)
+
+    def off_scatter(t):
+        at = pl.multiple_of(lax.rem(t, Q) * piece, piece)
+        return remote(off_part.at[lax.div(t, Q), pl.ds(at, piece)], off_got.at[g],
+                      off_s.at[t], off_r.at[g], dev(t, core))
+
+    def off_arrival(p):
+        return remote(off_part.at[0, pl.ds(0, piece)], off_got.at[p],
+                      off_s.at[p], off_r.at[p], dev(p, core))
+
+    others(G, g, lambda t: off_scatter(t).start())
+
+    others(Q, q, lambda p: own_gathered(p).wait_recv())
+
+    def own_forward(first):
+        place = own_amp.at[pl.ds(first, TS)]
+        return remote(place, place, fw_s.at[0], fw_r.at[0], sibling)
+
+    own_forward(mine).start()
+
+    def add_off(i, total):
+        p = lax.rem(g + i, G)
+        off_arrival(p).wait_recv()
+        return total + off_got[p].astype(F32)
+
+    off_mine = off_core[pl.ds(at_q, piece), pl.ds(pl.multiple_of(j * TS, TS), TS)]
+    off_total = lax.fori_loop(1, G, add_off, off_mine)
+    row_e = down(energy[pl.ds(core, 1), :])
+    row_s = scale(core)
+    col_e = energy[pl.ds(2 + j, 1), :]
+    col_s = scale(2 + j)
+    denominator = row_e + col_e
+    stage[0] = (off_total * (col_s * col_s) * row_s / denominator).astype(BF16)
+    stage[1] = (off_total * (row_s * row_s) * col_s / denominator).astype(BF16)
+
+    def off_gather(t):
+        return remote(stage.at[lax.div(t, Q)], off_amp.at[j, own_rows],
+                      offa_s.at[t], offa_r.at[g], dev(t, core))
+
+    def off_gathered(p):
+        at = pl.multiple_of(core * TS + lax.rem(p, Q) * piece, piece)
+        return remote(stage.at[0], off_amp.at[lax.div(p, Q), pl.ds(at, piece)],
+                      offa_s.at[p], offa_r.at[p], dev(p, core))
+
+    others(G, g, lambda t: off_gather(t).start())
+    off_amp[j, own_rows, :] = stage[j]
+
+    others(G, g, lambda p: off_gathered(p).wait_recv())
+
+    def off_forward(h, first):
+        place = off_amp.at[h, pl.ds(first, TS)]
+        return remote(place, place, fw_s.at[1 + h], fw_r.at[1 + h], sibling)
+
+    for h in range(2):
+        off_forward(h, mine).start()
+    own_forward(theirs).wait_recv()
+    got_b(1).wait_recv()
+    for h in range(2):
+        off_forward(h, theirs).wait_recv()
+
+    @pl.when(j == 0)
+    def _():
+        out_ref[...] = (nn_dot(b_ref[...], own_amp[...])
+                        + nt_dot(other[:, :TS], off_amp[0])
+                        + nt_dot(other[:, TS:], off_amp[1])).astype(BF16)
+
+    @pl.when(j == 1)
+    def _():
+        for h in range(2):
+            cols = slice(h * TS, (h + 1) * TS)
+            out_ref[:, cols] = (nn_dot(b_ref[...], own_amp[:, cols])
+                                + nn_dot(other[...], off_amp[h])).astype(BF16)
+
+    send_b(1).wait_send()
+    core_copy(0, own_c, own_core).wait_send()
+    core_copy(1, off_c, off_core).wait_send()
+    others(Q, q, lambda t: own_scatter(t).wait_send())
+    others(Q, q, lambda t: own_gather(t).wait_send())
+    others(G, g, lambda t: off_scatter(t).wait_send())
+    others(G, g, lambda t: off_gather(t).wait_send())
+    own_forward(mine).wait_send()
+    for h in range(2):
+        off_forward(h, mine).wait_send()
+
+
+def pair_body(Q, three_index, occupied_energy, virtual_energy, tile_occupied, tile_virtual,
+              tile_exponent):
+    rows, width = three_index.shape
+    piece = TS // Q
+    G = 2 * Q
+    vmem = pl.BlockSpec(memory_space=pltpu.VMEM)
+    smem = pl.BlockSpec(memory_space=pltpu.SMEM)
+    dma = pltpu.SemaphoreType.DMA
+    flops = 2 * rows * width * width * 4
+    return pl.pallas_call(
+        functools.partial(kernel, Q),
+        out_shape=jax.ShapeDtypeStruct((rows, width), BF16),
+        in_specs=[vmem, vmem, smem, smem, smem, smem],
+        out_specs=vmem,
+        scratch_shapes=[
+            pltpu.VMEM((rows, width), BF16),
+            pltpu.VMEM((width, width), F32),
+            pltpu.VMEM((width, width), F32),
+            pltpu.VMEM((TS, width), F32),
+            pltpu.VMEM((TS, width), F32),
+            pltpu.VMEM((TS, width), BF16),
+            pltpu.VMEM((2, TS, TS), BF16),
+            pltpu.VMEM((Q, piece, width), BF16),
+            pltpu.VMEM((G, piece, TS), BF16),
+            pltpu.VMEM((width, width), BF16),
+            pltpu.VMEM((2, width, TS), BF16),
+            pltpu.VMEM((2, piece, TS), BF16),
+            pltpu.VMEM((8, TS), F32),
+            dma((2,)), dma((2,)),
+            dma((2,)), dma((2,)),
+            dma((Q,)), dma((Q,)),
+            dma((G,)), dma((G,)),
+            dma((Q,)), dma((Q,)),
+            dma((G,)), dma((G,)),
+            dma((3,)), dma((3,)),
+        ],
+        compiler_params=pltpu.CompilerParams(
+            collective_id=0, has_side_effects=True, vmem_limit_bytes=32 * 1024 * 1024
+        ),
+        cost_estimate=pl.CostEstimate(
+            flops=flops, bytes_accessed=4 * rows * width, transcendentals=0
+        ),
+    )(three_index, virtual_energy.reshape(VT, TS), occupied_energy, tile_occupied, tile_virtual,
+      tile_exponent)
+
+
 def solution(mesh):
     placed = (P("aux", "pair"), P(), P(), P(), P(), P())
+    Q = mesh.shape["aux"] // 2
+
+    def body(*args):
+        if mesh.shape["pair"] == 2 and Q == 8 and args[0].shape[1] == 2 * TS:
+            return pair_body(Q, *args)
+        return general_body(*args)
+
     return jax.shard_map(
         body, mesh=mesh, in_specs=placed, out_specs=P("aux", "pair"), check_vma=False
     )

time: 124 us -> 31.8 us (0.26)
  the two profiles are of different devices: /device:TPU:0 before, /device:TPU:1 now
where the time goes in v1:
time: 31.8 us; the launch traced here: 31.5 us
  Pallas kernels  27.5 us (86%)
  local copies, waits for them, and re-layouts  4.01 us (13%)
    pallas_call x1, Pallas kernels, pair_body(): pl.pallas_call(functools.partial(kernel, Q), out_shape=jax.ShapeDtypeStru...  27.5 us
    unnamed x13, local copies, waits for them, and re-layouts  4.01 us

profile of v1, /device:TPU:1, one launch (start us, length us, event | category | flops | bytes accessed | tf_op | source)
XLA Modules:
  0.0 31.5 jit_solution(11256859633694689119)
XLA Ops:
  0.0 0.0 copy-start.4
  0.0 0.0 copy-start.3
  0.0 0.0 copy-start.2
  0.0 0.6 %copy-done.4 = s32[4]{0:T(128)S(1)} copy-done((s32[4]{0:T(128)S(1)}, s32[4]{0:T(128)}, u32[]{:S(2)}) %copy-start.4) | copy-done | bytes 40
  0.7 0.0 copy-done.3
  0.7 0.0 copy-done.2
  0.7 0.0 copy-start
  0.7 1.0 %copy-done = bf16[896,256]{1,0:T(8,128)(2,1)S(1)} copy-done((bf16[896,256]{1,0:T(8,128)(2,1)S(1)}, bf16[896,256]{1,0:T(8,128)(2,1)}, u32[]{:S(2)}) %copy-start) | copy-done | bytes 458776
  1.7 0.0 copy-start.1
  1.7 0.9 %copy-done.1 = f32[20096]{0:T(1024)S(1)} copy-done((f32[20096]{0:T(1024)S(1)}, f32[20096]{0:T(1024)}, u32[]{:S(2)}) %copy-start.1) | copy-done | bytes 80408
  2.6 0.0 copy-start.5
  2.6 0.7 %copy-done.5 = s32[4]{0:T(128)S(1)} copy-done((s32[4]{0:T(128)S(1)}, s32[4]{0:T(128)}, u32[]{:S(2)}) %copy-start.5) | copy-done | bytes 40
  3.2 27.5 %shard_map.64 = bf16[896,256]{1,0:T(8,128)(2,1)S(1)} custom-call(bf16[896,256]{1,0:T(8,128)(2,1)S(1)} %copy-done, f32[157,128]{1,0:T(8,128)S(1)} %bitcast.1, f32[64]{0:T(128)S(1)} %copy-done.2, s32[4]{0:T(128)S(1)} %copy-done.3, s32[4]{0:T(128)S(1)} %copy-done.4, s32[4]{0:T(128)S(1)} %copy-done.5), custom_call_target="tpu_custom_call" | custom-call | flops 469762048 | bytes 917504 | tf_op jit(solution)/shard_map/pallas_call | solution.py:295
  30.8 0.8 %copy.8 = bf16[896,256]{1,0:T(8,128)(2,1)} copy(bf16[896,256]{1,0:T(8,128)(2,1)S(1)} %shard_map.64) | data formatting | bytes 917504
Async XLA Ops:
  0.0 0.7 %copy-start.4 = (s32[4]{0:T(128)S(1)}, s32[4]{0:T(128)}, u32[]{:S(2)}) copy-start(s32[4]{0:T(128)} %tv_ref.1) | copy-start | bytes 52
  0.0 0.7 %copy-start.3 = (s32[4]{0:T(128)S(1)}, s32[4]{0:T(128)}, u32[]{:S(2)}) copy-start(s32[4]{0:T(128)} %to_ref.1) | copy-start | bytes 52
  0.0 0.7 %copy-start.2 = (f32[64]{0:T(128)S(1)}, f32[64]{0:T(128)}, u32[]{:S(2)}) copy-start(f32[64]{0:T(128)} %occ_ref.1) | copy-start | bytes 772
  0.7 1.0 %copy-start = (bf16[896,256]{1,0:T(8,128)(2,1)S(1)}, bf16[896,256]{1,0:T(8,128)(2,1)}, u32[]{:S(2)}) copy-start(bf16[896,256]{1,0:T(8,128)(2,1)} %b_ref.1) | copy-start | bytes 1376260
  1.7 0.9 %copy-start.1 = (f32[20096]{0:T(1024)S(1)}, f32[20096]{0:T(1024)}, u32[]{:S(2)}) copy-start(f32[20096]{0:T(1024)} %param.8) | copy-start | bytes 241156
  2.6 0.7 %copy-start.5 = (s32[4]{0:T(128)S(1)}, s32[4]{0:T(128)}, u32[]{:S(2)}) copy-start(s32[4]{0:T(128)} %te_ref.1) | copy-start | bytes 52

commit v2 on v1

v2 whole, which is shorter than its diff:
```python
import functools

import jax
import jax.numpy as jnp
from jax import lax
from jax.experimental import pallas as pl
from jax.experimental.pallas import tpu as pltpu
from jax.sharding import PartitionSpec as P

TS = 128
VT = 157
F32 = jnp.float32
BF16 = jnp.bfloat16
MESH = pl.DeviceIdType.MESH
VMEM_LIMIT = 60 * 1024 * 1024


def column_scale(tile_exponent):
    factor = jnp.where(tile_exponent == -1, 0.5, jnp.where(tile_exponent == 1, 2.0, 1.0)).astype(
        jnp.float32
    )
    return jnp.repeat(factor, TS)


def column_energy(occupied_energy, virtual_energy, tile_occupied, tile_virtual):
    virtual_cols = virtual_energy.reshape(VT, TS)[tile_virtual].reshape(-1)
    occupied_cols = jnp.repeat(occupied_energy[tile_occupied], TS)
    return virtual_cols - occupied_cols


def make_amplitude(coulomb, row_energy, row_scale, own_energy, own_scale):
    return (
        coulomb
        * (row_scale * row_scale)[:, None]
        * own_scale[None, :]
        / (row_energy[:, None] + own_energy[None, :])
    ).astype(jnp.bfloat16)


def general_body(
    three_index, occupied_energy, virtual_energy, tile_occupied, tile_virtual, tile_exponent
):
    width_local = three_index.shape[1]
    col_scale = column_scale(tile_exponent)
    col_energy = column_energy(occupied_energy, virtual_energy, tile_occupied, tile_virtual)
    offset = lax.axis_index("pair") * width_local
    own_energy = lax.dynamic_slice_in_dim(col_energy, offset, width_local)
    own_scale = lax.dynamic_slice_in_dim(col_scale, offset, width_local)
    contract = (((0,), (0,)), ((), ()))
    gathered = lax.all_gather(three_index, "pair", axis=1, tiled=True)
    coulomb = lax.dot_general(gathered, three_index, contract, preferred_element_type=jnp.float32)
    summed = lax.psum(coulomb, "aux")
    amplitude = make_amplitude(summed, col_energy, col_scale, own_energy, own_scale)
    result = jnp.dot(gathered, amplitude, preferred_element_type=jnp.float32)
    return result.astype(jnp.bfloat16)


def tn_dot(a, b):
    return lax.dot_general(a, b, (((0,), (0,)), ((), ())), preferred_element_type=F32)


def nt_dot(a, b):
    return lax.dot_general(a, b, (((1,), (1,)), ((), ())), preferred_element_type=F32)


def nn_dot(a, b):
    return jnp.dot(a, b, preferred_element_type=F32)


def kernel(
    Q, b_hbm, ve_hbm, occ_hbm, to_hbm, tv_hbm, te_hbm, out_ref,
    b_ref, ve_ref, occ_ref, to_ref, tv_ref, te_ref,
    other, own_send, own_sum, own_core, off_send, off_sum, off_core, own_part, off_part,
    own_got, off_got, own_amp, off_amp, stage, energy,
    load, b_s, b_r, core_s, core_r, own_s, own_r, off_s, off_r, owna_s, owna_r, offa_s, offa_r,
    fw_s, fw_r,
):
    rows = b_ref.shape[0]
    half = rows // 2
    piece = TS // Q
    aux = lax.axis_index("aux")
    j = lax.axis_index("pair")
    core = lax.rem(aux, 2)
    q = lax.div(aux, 2)
    G = 2 * Q
    g = j * Q + q

    def dev(chip, which):
        return {"aux": 2 * lax.rem(chip, Q) + which, "pair": lax.div(chip, Q)}

    def remote(src, dst, send, recv, target):
        return pltpu.make_async_remote_copy(
            src_ref=src, dst_ref=dst, send_sem=send, recv_sem=recv,
            device_id=target, device_id_type=MESH,
        )

    sibling = dev(g, 1 - core)
    across = dev(lax.rem(g + Q, G), core)
    chips = [lax.rem(g + i, G) for i in range(1, G)]
    own_chips = [lax.rem(q + i, Q) for i in range(1, Q)]

    loads = [
        pltpu.make_async_copy(src, dst, load.at[k])
        for k, (src, dst) in enumerate([
            (b_hbm, b_ref), (ve_hbm, ve_ref), (occ_hbm, occ_ref),
            (to_hbm, to_ref), (tv_hbm, tv_ref), (te_hbm, te_ref),
        ])
    ]
    barrier = pltpu.get_barrier_semaphore()
    pl.semaphore_signal(barrier, inc=1, device_id=sibling, device_id_type=MESH)
    for t in chips:
        pl.semaphore_signal(barrier, inc=1, device_id=dev(t, core), device_id_type=MESH)
    for one in loads:
        one.start()

    mine = pl.multiple_of(core * TS, TS)
    theirs = pl.multiple_of((1 - core) * TS, TS)
    at_q = pl.multiple_of(q * piece, piece)
    own_rows = pl.ds(pl.multiple_of(core * TS + q * piece, piece), piece)
    here = pl.multiple_of((1 - j) * half, half)
    away = pl.multiple_of(j * half, half)
    half_rows = [(away, here), (here, away)]

    def send_b(k):
        at = pl.ds(half_rows[k][0], half)
        return remote(b_hbm.at[at], other.at[at], b_s.at[k], b_r.at[k], across)

    def got_b(k):
        at = pl.ds(half_rows[k][1], half)
        return remote(b_hbm.at[at], other.at[at], b_s.at[k], b_r.at[k], across)

    pl.semaphore_wait(barrier, G)
    send_b(0).start()

    own_core_copy = remote(own_send, own_core, core_s.at[0], core_r.at[0], sibling)
    loads[0].wait()
    own_send[...] = tn_dot(b_ref[:, pl.ds(theirs, TS)], b_ref[...])
    own_core_copy.start()
    own_sum[...] = tn_dot(b_ref[:, pl.ds(mine, TS)], b_ref[...])

    for one in loads[1:]:
        one.wait()
    for t in range(4):
        energy[t:t + 1, :] = ve_ref[pl.ds(tv_ref[t], 1), :] - occ_ref[to_ref[t]]

    def scale(t):
        e = te_ref[t]
        return jnp.where(e == -1, 0.5, jnp.where(e == 1, 2.0, 1.0)).astype(F32)

    def down(row):
        shape = (piece, TS)
        pick = lax.broadcasted_iota(jnp.int32, shape, 1) == (
            lax.broadcasted_iota(jnp.int32, shape, 0) + q * piece)
        return jnp.sum(jnp.where(pick, row, 0.0), axis=1, keepdims=True)

    own_got[q] = jnp.zeros(own_got.shape[1:], BF16)
    off_got[g] = jnp.zeros(off_got.shape[1:], BF16)

    own_core_copy.wait_recv()
    own_sum[...] += own_core[...]
    own_part[...] = own_sum[...].astype(BF16)
    for t in own_chips:
        remote(own_part.at[pl.ds(pl.multiple_of(t * piece, piece), piece)], own_got.at[q],
               own_s, own_r, dev(j * Q + t, core)).start()

    own_bytes = own_got.at[pl.ds(0, Q - 1)]
    own_all = remote(own_bytes, own_bytes, own_s, own_r, sibling)
    own_all.wait_recv()
    own_total = own_sum[pl.ds(at_q, piece), :]
    for p in range(Q):
        own_total = own_total + own_got[p].astype(F32)
    row_e = down(energy[pl.ds(2 * j + core, 1), :])
    row_s = scale(2 * j + core)
    for h in range(2):
        cols = slice(h * TS, (h + 1) * TS)
        col_e = energy[pl.ds(2 * j + h, 1), :]
        col_s = scale(2 * j + h)
        own_amp[own_rows, cols] = (
            own_total[:, cols] * (row_s * row_s) * col_s / (row_e + col_e)
        ).astype(BF16)
    for t in own_chips:
        remote(own_amp.at[own_rows], own_amp.at[own_rows],
               owna_s, owna_r, dev(j * Q + t, core)).start()

    off_core_copy = remote(off_send, off_core, core_s.at[1], core_r.at[1], sibling)
    here_rows = pl.ds(here, half)
    got_b(0).wait_recv()

    @pl.when(j == 0)
    def _():
        off_send[...] = tn_dot(b_ref[here_rows, pl.ds(theirs, TS)], other[here_rows, :])

    @pl.when(j == 1)
    def _():
        off_send[...] = tn_dot(other[here_rows, pl.ds(theirs, TS)], b_ref[here_rows, :])

    off_core_copy.start()

    @pl.when(j == 0)
    def _():
        off_sum[...] = tn_dot(b_ref[here_rows, pl.ds(mine, TS)], other[here_rows, :])

    @pl.when(j == 1)
    def _():
        off_sum[...] = tn_dot(other[here_rows, pl.ds(mine, TS)], b_ref[here_rows, :])

    off_core_copy.wait_recv()
    off_sum[...] += off_core[...]
    for h in range(2):
        off_part[h] = off_sum[:, h * TS:(h + 1) * TS].astype(BF16)
    for t in chips:
        at = pl.multiple_of(lax.rem(t, Q) * piece, piece)
        remote(off_part.at[lax.div(t, Q), pl.ds(at, piece)], off_got.at[g],
               off_s, off_r, dev(t, core)).start()
    send_b(0).wait_send()
    send_b(1).start()

    own_amp_bytes = own_amp.at[pl.ds(0, (Q - 1) * piece)]
    own_amp_all = remote(own_amp_bytes, own_amp_bytes, owna_s, owna_r, sibling)
    own_amp_all.wait_recv()

    def own_forward(first):
        place = own_amp.at[pl.ds(first, TS)]
        return remote(place, place, fw_s.at[0], fw_r.at[0], sibling)

    own_forward(mine).start()
    own_core_copy.wait_send()
    own_all.wait_send()
    own_amp_all.wait_send()

    row_e = down(energy[pl.ds(core, 1), :])
    row_s = scale(core)
    col_e = energy[pl.ds(2 + j, 1), :]
    col_s = scale(2 + j)
    denominator = row_e + col_e
    off_bytes = off_got.at[pl.ds(0, G - 1)]
    off_all = remote(off_bytes, off_bytes, off_s, off_r, sibling)
    off_all.wait_recv()
    off_total = off_sum[pl.ds(at_q, piece), pl.ds(pl.multiple_of(j * TS, TS), TS)]
    for p in range(G):
        off_total = off_total + off_got[p].astype(F32)
    stage[0] = (off_total * (col_s * col_s) * row_s / denominator).astype(BF16)
    stage[1] = (off_total * (row_s * row_s) * col_s / denominator).astype(BF16)
    for t in chips:
        remote(stage.at[lax.div(t, Q)], off_amp.at[j, own_rows],
               offa_s, offa_r, dev(t, core)).start()
    off_amp[j, own_rows, :] = stage[j]
    off_core_copy.wait_send()
    off_all.wait_send()

    off_amp_bytes = off_amp.at[0, pl.ds(0, (G - 1) * piece)]
    off_amp_all = remote(off_amp_bytes, off_amp_bytes, offa_s, offa_r, sibling)
    off_amp_all.wait_recv()

    def off_forward(h, first):
        place = off_amp.at[h, pl.ds(first, TS)]
        return remote(place, place, fw_s.at[1 + h], fw_r.at[1 + h], sibling)

    for h in range(2):
        off_forward(h, mine).start()
    off_amp_all.wait_send()
    own_forward(mine).wait_send()
    own_forward(theirs).wait_recv()
    send_b(1).wait_send()
    got_b(1).wait_recv()
    for h in range(2):
        off_forward(h, theirs).wait_recv()

    @pl.when(j == 0)
    def _():
        out_ref[...] = (nn_dot(b_ref[...], own_amp[...])
                        + nt_dot(other[:, :TS], off_amp[0])
                        + nt_dot(other[:, TS:], off_amp[1])).astype(BF16)

    @pl.when(j == 1)
    def _():
        for h in range(2):
            cols = slice(h * TS, (h + 1) * TS)
            out_ref[:, cols] = (nn_dot(b_ref[...], own_amp[:, cols])
                                + nn_dot(other[...], off_amp[h])).astype(BF16)

    for h in range(2):
        off_forward(h, mine).wait_send()


def pair_body(Q, three_index, occupied_energy, virtual_energy, tile_occupied, tile_virtual,
              tile_exponent):
    rows, width = three_index.shape
    piece = TS // Q
    G = 2 * Q
    hbm = pl.BlockSpec(memory_space=pl.ANY)
    dma = pltpu.SemaphoreType.DMA
    flops = 2 * rows * width * width * 4
    return pl.pallas_call(
        functools.partial(kernel, Q),
        out_shape=jax.ShapeDtypeStruct((rows, width), BF16),
        in_specs=[hbm] * 6,
        out_specs=pl.BlockSpec(memory_space=pltpu.VMEM),
        scratch_shapes=[
            pltpu.VMEM((rows, width), BF16),
            pltpu.VMEM((VT, TS), F32),
            pltpu.SMEM(occupied_energy.shape, F32),
            pltpu.SMEM(tile_occupied.shape, jnp.int32),
            pltpu.SMEM(tile_virtual.shape, jnp.int32),
            pltpu.SMEM(tile_exponent.shape, jnp.int32),
            pltpu.VMEM((rows, width), BF16),
            pltpu.VMEM((TS, width), F32),
            pltpu.VMEM((TS, width), F32),
            pltpu.VMEM((TS, width), F32),
            pltpu.VMEM((TS, width), F32),
            pltpu.VMEM((TS, width), F32),
            pltpu.VMEM((TS, width), F32),
            pltpu.VMEM((TS, width), BF16),
            pltpu.VMEM((2, TS, TS), BF16),
            pltpu.VMEM((Q, piece, width), BF16),
            pltpu.VMEM((G, piece, TS), BF16),
            pltpu.VMEM((width, width), BF16),
            pltpu.VMEM((2, width, TS), BF16),
            pltpu.VMEM((2, piece, TS), BF16),
            pltpu.VMEM((8, TS), F32),
            dma((6,)),
            dma((2,)), dma((2,)),
            dma((2,)), dma((2,)),
            dma, dma, dma, dma, dma, dma, dma, dma,
            dma((3,)), dma((3,)),
        ],
        compiler_params=pltpu.CompilerParams(
            collective_id=0, has_side_effects=True, vmem_limit_bytes=VMEM_LIMIT
        ),
        cost_estimate=pl.CostEstimate(
            flops=flops, bytes_accessed=4 * rows * width, transcendentals=0
        ),
    )(three_index, virtual_energy.reshape(VT, TS), occupied_energy, tile_occupied, tile_virtual,
      tile_exponent)


def solution(mesh):
    placed = (P("aux", "pair"), P(), P(), P(), P(), P())
    Q = mesh.shape["aux"] // 2

    def body(*args):
        if mesh.shape["pair"] == 2 and Q == 8 and args[0].shape[1] == 2 * TS:
            return pair_body(Q, *args)
        return general_body(*args)

    return jax.shard_map(
        body, mesh=mesh, in_specs=placed, out_specs=P("aux", "pair"), check_vma=False
    )
```

time: 31.8 us -> 27.7 us (0.87)
  local copies, waits for them, and re-layouts: 4.01 us -> 1.82 us
  Pallas kernels: 27.5 us -> 25.7 us
    unnamed x13 -> x1, local copies, waits for them, and re-layouts: 4.01 us -> 1.82 us
    pallas_call x1, Pallas kernels: 27.5 us -> 25.7 us  [pair_body(): pl.pallas_call(functools.partial(kernel, Q), out_shape=jax.ShapeDtypeStru...]
where the time goes in v2:
time: 27.7 us; the launch traced here: 27.5 us
  Pallas kernels  25.7 us (93%)
  local copies, waits for them, and re-layouts  1.82 us (7%)
    pallas_call x1, Pallas kernels, pair_body(): pl.pallas_call(functools.partial(kernel, Q), out_shape=jax.ShapeDtypeStru...  25.7 us
    unnamed x1, local copies, waits for them, and re-layouts  1.82 us

profile of v2, /device:TPU:1, one launch (start us, length us, event | category | flops | bytes accessed | tf_op | source)
XLA Modules:
  0.0 27.5 jit_solution(4515639055242726670)
XLA Ops:
  0.0 25.7 %shard_map.64 = bf16[896,256]{1,0:T(8,128)(2,1)} custom-call(bf16[896,256]{1,0:T(8,128)(2,1)} %b_hbm.1, f32[157,128]{1,0:T(8,128)} %bitcast.1, f32[64]{0:T(128)} %occ_hbm.1, s32[4]{0:T(128)} %to_hbm.1, s32[4]{0:T(128)} %tv_hbm.1, s32[4]{0:T(128)} %te_hbm.1), custom_call_target="tpu_custom_call" | custom-call | flops 469762048 | bytes 917504 | tf_op jit(solution)/shard_map/pallas_call | solution.py:294
  25.7 1.8 %copy.8 = bf16[896,256]{1,0:T(8,128)(2,1)} copy(bf16[896,256]{1,0:T(8,128)(2,1)} %shard_map.64) | data formatting | bytes 917504

commit v3 on v0

--- a/solution.py
+++ b/solution.py
@@ -1,10 +1,18 @@
+import functools
+
 import jax
 import jax.numpy as jnp
 from jax import lax
+from jax.experimental import pallas as pl
+from jax.experimental.pallas import tpu as pltpu
 from jax.sharding import PartitionSpec as P
 
 TS = 128
 VT = 157
+F32 = jnp.float32
+BF16 = jnp.bfloat16
+MESH = pl.DeviceIdType.MESH
+VMEM_LIMIT = 60 * 1024 * 1024
 
 
 def column_scale(tile_exponent):
@@ -29,7 +37,9 @@
     ).astype(jnp.bfloat16)
 
 
-def body(three_index, occupied_energy, virtual_energy, tile_occupied, tile_virtual, tile_exponent):
+def general_body(
+    three_index, occupied_energy, virtual_energy, tile_occupied, tile_virtual, tile_exponent
+):
     width_local = three_index.shape[1]
     col_scale = column_scale(tile_exponent)
     col_energy = column_energy(occupied_energy, virtual_energy, tile_occupied, tile_virtual)
@@ -45,8 +55,289 @@
     return result.astype(jnp.bfloat16)
 
 
+def tn_dot(a, b):
+    return lax.dot_general(a, b, (((0,), (0,)), ((), ())), preferred_element_type=F32)
+
+
+def nt_dot(a, b):
+    return lax.dot_general(a, b, (((1,), (1,)), ((), ())), preferred_element_type=F32)
+
+
+def nn_dot(a, b):
+    return jnp.dot(a, b, preferred_element_type=F32)
+
+
+def kernel(
+    W, Z, b_hbm, ve_hbm, occ_hbm, to_hbm, tv_hbm, te_hbm, total_ref, other, off_amp,
+    b_ref, ve_ref, occ_ref, to_ref, tv_ref, te_ref,
+    own_sum, off_sum, own_part, off_part, own_got, off_got, own_line, off_line,
+    own_line_got, off_line_got, own_amp, stage, energy,
+    load, b_s, b_r, sems,
+):
+    rows, width = b_ref.shape
+    half = rows // 2
+    S = 2 * W
+    own_piece = width // W
+    off_piece = width // S
+    aux = lax.axis_index("aux")
+    j = lax.axis_index("pair")
+    z = lax.div(aux, W)
+    w = lax.rem(aux, W)
+    s = j * W + w
+
+    def dev(line, place):
+        return {"aux": line * W + lax.rem(place, W), "pair": lax.div(place, W)}
+
+    def remote(src, dst, send, recv, target):
+        return pltpu.make_async_remote_copy(
+            src_ref=src, dst_ref=dst, send_sem=send, recv_sem=recv,
+            device_id=target, device_id_type=MESH,
+        )
+
+    across = dev(z, lax.rem(s + W, S))
+    plane = [lax.rem(s + i, S) for i in range(1, S)]
+    side = [lax.rem(w + i, W) for i in range(1, W)]
+    line = [lax.rem(z + i, Z) for i in range(1, Z)]
+
+    loads = [
+        pltpu.make_async_copy(src, dst, load.at[k])
+        for k, (src, dst) in enumerate([
+            (b_hbm, b_ref), (ve_hbm, ve_ref), (occ_hbm, occ_ref),
+            (to_hbm, to_ref), (tv_hbm, tv_ref), (te_hbm, te_ref),
+        ])
+    ]
+    barrier = pltpu.get_barrier_semaphore()
+    for k in plane:
+        pl.semaphore_signal(barrier, inc=1, device_id=dev(z, k), device_id_type=MESH)
+    for k in line:
+        pl.semaphore_signal(barrier, inc=1, device_id=dev(k, s), device_id_type=MESH)
+    for one in loads:
+        one.start()
+
+    here = pl.multiple_of((1 - j) * half, half)
+    away = pl.multiple_of(j * half, half)
+    half_rows = [(away, here), (here, away)]
+    own_at = pl.multiple_of(w * own_piece, own_piece)
+    off_at = pl.multiple_of(s * off_piece, off_piece)
+
+    def send_b(k):
+        at = pl.ds(half_rows[k][0], half)
+        return remote(b_hbm.at[at], other.at[at], b_s.at[k], b_r.at[k], across)
+
+    def got_b(k):
+        at = pl.ds(half_rows[k][1], half)
+        return remote(b_hbm.at[at], other.at[at], b_s.at[k], b_r.at[k], across)
+
+    def group(k, ref):
+        return remote(ref, ref, sems.at[2 * k], sems.at[2 * k + 1], across)
+
+    def scale(t):
+        e = te_ref[t]
+        return jnp.where(e == -1, 0.5, jnp.where(e == 1, 2.0, 1.0)).astype(F32)
+
+    def down(row, first, count):
+        shape = (count, TS)
+        pick = lax.broadcasted_iota(jnp.int32, shape, 1) == (
+            lax.broadcasted_iota(jnp.int32, shape, 0) + first)
+        return jnp.sum(jnp.where(pick, row, 0.0), axis=1, keepdims=True)
+
+    pl.semaphore_wait(barrier, S - 1 + Z - 1)
+    send_b(0).start()
+
+    loads[0].wait()
+    own_sum[...] = tn_dot(b_ref[...], b_ref[...])
+    own_part[...] = own_sum[...].astype(BF16)
+    for k in side:
+        remote(own_part.at[pl.ds(pl.multiple_of(k * own_piece, own_piece), own_piece)],
+               own_got.at[w], sems.at[0], sems.at[1], dev(z, j * W + k)).start()
+
+    for one in loads[1:]:
+        one.wait()
+    for t in range(4):
+        energy[t:t + 1, :] = ve_ref[pl.ds(tv_ref[t], 1), :] - occ_ref[to_ref[t]]
+    own_got[w] = jnp.zeros(own_got.shape[1:], BF16)
+    off_got[s] = jnp.zeros(off_got.shape[1:], BF16)
+    own_line_got[z] = jnp.zeros(own_line_got.shape[1:], BF16)
+    off_line_got[z] = jnp.zeros(off_line_got.shape[1:], BF16)
+
+    own_scattered = group(0, own_got.at[pl.ds(0, W - 1)])
+    own_scattered.wait_recv()
+    own_total = own_sum[pl.ds(own_at, own_piece), :]
+    for k in range(W):
+        own_total = own_total + own_got[k].astype(F32)
+    own_line[...] = own_total.astype(BF16)
+    for k in line:
+        remote(own_line, own_line_got.at[z], sems.at[2], sems.at[3], dev(k, s)).start()
+
+    here_rows = pl.ds(here, half)
+    got_b(0).wait_recv()
+
+    @pl.when(j == 0)
+    def _():
+        off_sum[...] = tn_dot(b_ref[here_rows, :], other[here_rows, :])
+
+    @pl.when(j == 1)
+    def _():
+        off_sum[...] = tn_dot(other[here_rows, :], b_ref[here_rows, :])
+
+    off_part[...] = off_sum[...].astype(BF16)
+    for k in plane:
+        remote(off_part.at[pl.ds(pl.multiple_of(k * off_piece, off_piece), off_piece)],
+               off_got.at[s], sems.at[6], sems.at[7], dev(z, k)).start()
+    send_b(0).wait_send()
+    send_b(1).start()
+
+    own_lined = group(1, own_line_got.at[pl.ds(0, Z - 1)])
+    own_lined.wait_recv()
+    for k in range(Z):
+        own_total = own_total + own_line_got[k].astype(F32)
+    tile = lax.div(own_at, TS)
+    row_e = down(energy[pl.ds(2 * j + tile, 1), :], lax.rem(own_at, TS), own_piece)
+    row_s = scale(2 * j + tile)
+    own_rows = pl.ds(own_at, own_piece)
+    for h in range(2):
+        cols = slice(h * TS, (h + 1) * TS)
+        col_e = energy[pl.ds(2 * j + h, 1), :]
+        col_s = scale(2 * j + h)
+        own_amp[own_rows, cols] = (
+            own_total[:, cols] * (row_s * row_s) * col_s / (row_e + col_e)
+        ).astype(BF16)
+    for k in side:
+        remote(own_amp.at[own_rows], own_amp.at[own_rows],
+               sems.at[4], sems.at[5], dev(z, j * W + k)).start()
+
+    off_scattered = group(3, off_got.at[pl.ds(0, S - 1)])
+    off_scattered.wait_recv()
+    off_total = off_sum[pl.ds(off_at, off_piece), :]
+    for k in range(S):
+        off_total = off_total + off_got[k].astype(F32)
+    off_line[...] = off_total.astype(BF16)
+    for k in line:
+        remote(off_line, off_line_got.at[z], sems.at[8], sems.at[9], dev(k, s)).start()
+
+    own_gathered = group(2, own_amp.at[pl.ds(0, (W - 1) * own_piece)])
+    own_gathered.wait_recv()
+    total_ref[...] = nn_dot(b_ref[...], own_amp[...])
+    own_scattered.wait_send()
+    own_lined.wait_send()
+    off_scattered.wait_send()
+
+    row_e = down(energy[pl.ds(j, 1), :], w * off_piece, off_piece)
+    row_s = scale(j)
+    off_lined = group(4, off_line_got.at[pl.ds(0, Z - 1)])
+    off_lined.wait_recv()
+    for k in range(Z):
+        off_total = off_total + off_line_got[k].astype(F32)
+    for h in range(2):
+        cols = slice(h * TS, (h + 1) * TS)
+        denominator = row_e + energy[2 + h:3 + h, :]
+        col_s = scale(2 + h)
+        value = off_total[:, cols]
+        stage[0, :, cols] = (value * (col_s * col_s) * row_s / denominator).astype(BF16)
+        stage[1, :, cols] = (value * (row_s * row_s) * col_s / denominator).astype(BF16)
+    off_rows = pl.ds(off_at, off_piece)
+    for k in plane:
+        remote(stage.at[lax.div(k, W)], off_amp.at[off_rows],
+               sems.at[10], sems.at[11], dev(z, k)).start()
+    off_amp[off_rows, :] = stage[j]
+    own_gathered.wait_send()
+    off_lined.wait_send()
+    send_b(1).wait_send()
+    got_b(1).wait_recv()
+    off_gathered = group(5, off_amp.at[pl.ds(0, (S - 1) * off_piece)])
+    off_gathered.wait_send()
+    off_gathered.wait_recv()
+
+
+def finish(total_ref, other, off_amp, out_ref):
+    j = lax.axis_index("pair")
+    count = out_ref.shape[0]
+    at = pl.ds(pl.multiple_of(pl.program_id(0) * count, count), count)
+
+    @pl.when(j == 0)
+    def _():
+        out_ref[...] = (total_ref[at, :] + nt_dot(other[at, :], off_amp[...])).astype(BF16)
+
+    @pl.when(j == 1)
+    def _():
+        out_ref[...] = (total_ref[at, :] + nn_dot(other[at, :], off_amp[...])).astype(BF16)
+
+
+def pair_body(W, Z, three_index, occupied_energy, virtual_energy, tile_occupied, tile_virtual,
+              tile_exponent):
+    rows, width = three_index.shape
+    S = 2 * W
+    own_piece = width // W
+    off_piece = width // S
+    hbm = pl.BlockSpec(memory_space=pltpu.HBM)
+    vmem = pl.BlockSpec(memory_space=pltpu.VMEM)
+    dma = pltpu.SemaphoreType.DMA
+    flops = 2 * rows * width * width
+    total, other, off_amp = pl.pallas_call(
+        functools.partial(kernel, W, Z),
+        out_shape=[
+            pltpu.VMEM((rows, width), F32),
+            pltpu.VMEM((rows, width), BF16),
+            pltpu.VMEM((width, width), BF16),
+        ],
+        in_specs=[hbm] * 6,
+        out_specs=[vmem] * 3,
+        scratch_shapes=[
+            pltpu.VMEM((rows, width), BF16),
+            pltpu.VMEM((VT, TS), F32),
+            pltpu.SMEM(occupied_energy.shape, F32),
+            pltpu.SMEM(tile_occupied.shape, jnp.int32),
+            pltpu.SMEM(tile_virtual.shape, jnp.int32),
+            pltpu.SMEM(tile_exponent.shape, jnp.int32),
+            pltpu.VMEM((width, width), F32),
+            pltpu.VMEM((width, width), F32),
+            pltpu.VMEM((width, width), BF16),
+            pltpu.VMEM((width, width), BF16),
+            pltpu.VMEM((W, own_piece, width), BF16),
+            pltpu.VMEM((S, off_piece, width), BF16),
+            pltpu.VMEM((own_piece, width), BF16),
+            pltpu.VMEM((off_piece, width), BF16),
+            pltpu.VMEM((Z, own_piece, width), BF16),
+            pltpu.VMEM((Z, off_piece, width), BF16),
+            pltpu.VMEM((width, width), BF16),
+            pltpu.VMEM((2, off_piece, width), BF16),
+            pltpu.VMEM((8, TS), F32),
+            dma((6,)),
+            dma((2,)), dma((2,)),
+            dma((12,)),
+        ],
+        compiler_params=pltpu.CompilerParams(
+            collective_id=0, has_side_effects=True, vmem_limit_bytes=VMEM_LIMIT
+        ),
+        cost_estimate=pl.CostEstimate(
+            flops=3 * flops, bytes_accessed=4 * rows * width, transcendentals=0
+        ),
+    )(three_index, virtual_energy.reshape(VT, TS), occupied_energy, tile_occupied, tile_virtual,
+      tile_exponent)
+    steps = 4
+    return pl.pallas_call(
+        finish,
+        grid=(steps,),
+        out_shape=jax.ShapeDtypeStruct((rows, width), BF16),
+        in_specs=[vmem] * 3,
+        out_specs=pl.BlockSpec((rows // steps, width), lambda i: (i, 0)),
+        compiler_params=pltpu.CompilerParams(vmem_limit_bytes=8 * 1024 * 1024),
+        cost_estimate=pl.CostEstimate(
+            flops=flops, bytes_accessed=2 * rows * width, transcendentals=0
+        ),
+    )(total, other, off_amp)
+
+
 def solution(mesh):
     placed = (P("aux", "pair"), P(), P(), P(), P(), P())
+    W = 4
+    Z = mesh.shape["aux"] // W
+
+    def body(*args):
+        if mesh.shape["pair"] == 2 and Z * W == 16 and args[0].shape[1] == 2 * TS:
+            return pair_body(W, Z, *args)
+        return general_body(*args)
+
     return jax.shard_map(
         body, mesh=mesh, in_specs=placed, out_specs=P("aux", "pair"), check_vma=False
     )

time: 124 us -> 25.7 us (0.21)
  waiting for transfers between devices: 88.2 us -> 0 us
  Pallas kernels: 0 us -> 25.6 us
  blocking collectives: 14.5 us -> 0 us
  between operations: 13.4 us -> 0.01 us
  local copies, waits for them, and re-layouts: 4.34 us -> 0 us
  matrix products: 3 us -> 0 us
    psum x1 -> x0, waiting for transfers between devices: 88.2 us -> none  [body(): summed = lax.psum(coulomb, 'aux')]
    pallas_call x0 -> x2, Pallas kernels: none -> 25.6 us  [the longest x1 23.6 us: pair_body(): pl.pallas_call(functools.partial(kernel, W, Z), out_shape=[pltpu.VMEM((ro...]
    all_gather x1 -> x0, blocking collectives: 14.5 us -> none  [body(): gathered = lax.all_gather(three_index, 'pair', axis=1, tiled=True)]
    dot_general x2 -> x0, matrix products: 3 us -> none  [the longest x1 1.73 us: body(): result = jnp.dot(gathered, amplitude, preferred_element_type=jnp.float32)]
    unnamed x12 -> x0, local copies, waits for them, and re-layouts: 1.93 us -> none
  transfers between devices with their start and end apart: 1 -> 0, of which waited for: 1 -> 0; matrix products, arithmetic and copies ran while one was open for 1% -> 0% of each run, Pallas kernels for 0% -> 0%
where the time goes in v3:
time: 25.7 us; the launch traced here: 25.6 us
  Pallas kernels  25.6 us (100%)
    pallas_call x1, Pallas kernels, pair_body(): pl.pallas_call(functools.partial(kernel, W, Z), out_shape=[pltpu.VMEM((ro...  23.6 us
    pallas_call x1, Pallas kernels, pair_body(): pl.pallas_call(finish, grid=(steps,), out_shape=jax.ShapeDtypeStruct((row...  2 us

profile of v3, /device:TPU:0, one launch (start us, length us, event | category | flops | bytes accessed | tf_op | source)
XLA Modules:
  0.0 25.6 jit_solution(855583411409848938)
XLA Ops:
  0.0 23.6 %shard_map.64 = (f32[896,256]{1,0:T(8,128)S(1)}, bf16[896,256]{1,0:T(8,128)(2,1)S(1)}, bf16[256,256]{1,0:T(8,128)(2,1)S(1)}) custom-call(bf16[896,256]{1,0:T(8,128)(2,1)} %b_hbm.1, f32[157,128]{1,0:T(8,128)} %bitcast.1, f32[64]{0:T(128)} %occ_hbm.1, s32[4]{0:T(128)} %to_hbm.1, s32[4]{0:T(128)} %tv_hbm.1, s32[4]{0:T(128)} %te_hbm.1), custom_call_target="tpu_custom_call" | custom-call | flops 352321536 | bytes 917504 | tf_op jit(solution)/shard_map/pallas_call | solution.py:276
  23.6 2.0 %shard_map.65 = bf16[896,256]{1,0:T(8,128)(2,1)} custom-call(f32[896,256]{1,0:T(8,128)S(1)} %get-tuple-element.8.total_ref, bf16[896,256]{1,0:T(8,128)(2,1)S(1)} %get-tuple-element.9.other, bf16[256,256]{1,0:T(8,128)(2,1)S(1)} %get-tuple-element.10.off_amp), custom_call_target="tpu_custom_call" | custom-call | flops 117440512 | bytes 458752 | tf_op jit(solution)/shard_map/pallas_call | solution.py:318

commit v4 on v3

--- a/solution.py
+++ b/solution.py
@@ -68,8 +68,8 @@
 
 
 def kernel(
-    W, Z, b_hbm, ve_hbm, occ_hbm, to_hbm, tv_hbm, te_hbm, total_ref, other, off_amp,
-    b_ref, ve_ref, occ_ref, to_ref, tv_ref, te_ref,
+    W, Z, b_hbm, ve_hbm, occ_hbm, to_hbm, tv_hbm, te_hbm, out_ref,
+    b_ref, ve_ref, occ_ref, to_ref, tv_ref, te_ref, own_product, other, off_amp,
     own_sum, off_sum, own_part, off_part, own_got, off_got, own_line, off_line,
     own_line_got, off_line_got, own_amp, stage, energy,
     load, b_s, b_r, sems,
@@ -170,6 +170,9 @@
         remote(own_line, own_line_got.at[z], sems.at[2], sems.at[3], dev(k, s)).start()
 
     here_rows = pl.ds(here, half)
+    away_rows = pl.ds(away, half)
+    send_b(0).wait_send()
+    send_b(1).start()
     got_b(0).wait_recv()
 
     @pl.when(j == 0)
@@ -184,8 +187,6 @@
     for k in plane:
         remote(off_part.at[pl.ds(pl.multiple_of(k * off_piece, off_piece), off_piece)],
                off_got.at[s], sems.at[6], sems.at[7], dev(z, k)).start()
-    send_b(0).wait_send()
-    send_b(1).start()
 
     own_lined = group(1, own_line_got.at[pl.ds(0, Z - 1)])
     own_lined.wait_recv()
@@ -217,7 +218,7 @@
 
     own_gathered = group(2, own_amp.at[pl.ds(0, (W - 1) * own_piece)])
     own_gathered.wait_recv()
-    total_ref[...] = nn_dot(b_ref[...], own_amp[...])
+    own_product[...] = nn_dot(b_ref[...], own_amp[...])
     own_scattered.wait_send()
     own_lined.wait_send()
     off_scattered.wait_send()
@@ -242,25 +243,22 @@
     off_amp[off_rows, :] = stage[j]
     own_gathered.wait_send()
     off_lined.wait_send()
-    send_b(1).wait_send()
-    got_b(1).wait_recv()
     off_gathered = group(5, off_amp.at[pl.ds(0, (S - 1) * off_piece)])
     off_gathered.wait_send()
     off_gathered.wait_recv()
 
-
-def finish(total_ref, other, off_amp, out_ref):
-    j = lax.axis_index("pair")
-    count = out_ref.shape[0]
-    at = pl.ds(pl.multiple_of(pl.program_id(0) * count, count), count)
-
-    @pl.when(j == 0)
-    def _():
-        out_ref[...] = (total_ref[at, :] + nt_dot(other[at, :], off_amp[...])).astype(BF16)
-
-    @pl.when(j == 1)
-    def _():
-        out_ref[...] = (total_ref[at, :] + nn_dot(other[at, :], off_amp[...])).astype(BF16)
+    for at, later in ((here_rows, False), (away_rows, True)):
+        if later:
+            send_b(1).wait_send()
+            got_b(1).wait_recv()
+
+        @pl.when(j == 0)
+        def _():
+            out_ref[at, :] = (own_product[at, :] + nt_dot(other[at, :], off_amp[...])).astype(BF16)
+
+        @pl.when(j == 1)
+        def _():
+            out_ref[at, :] = (own_product[at, :] + nn_dot(other[at, :], off_amp[...])).astype(BF16)
 
 
 def pair_body(W, Z, three_index, occupied_energy, virtual_energy, tile_occupied, tile_virtual,
@@ -273,15 +271,11 @@
     vmem = pl.BlockSpec(memory_space=pltpu.VMEM)
     dma = pltpu.SemaphoreType.DMA
     flops = 2 * rows * width * width
-    total, other, off_amp = pl.pallas_call(
+    return pl.pallas_call(
         functools.partial(kernel, W, Z),
-        out_shape=[
-            pltpu.VMEM((rows, width), F32),
-            pltpu.VMEM((rows, width), BF16),
-            pltpu.VMEM((width, width), BF16),
-        ],
+        out_shape=pltpu.VMEM((rows, width), BF16),
         in_specs=[hbm] * 6,
-        out_specs=[vmem] * 3,
+        out_specs=vmem,
         scratch_shapes=[
             pltpu.VMEM((rows, width), BF16),
             pltpu.VMEM((VT, TS), F32),
@@ -289,6 +283,9 @@
             pltpu.SMEM(tile_occupied.shape, jnp.int32),
             pltpu.SMEM(tile_virtual.shape, jnp.int32),
             pltpu.SMEM(tile_exponent.shape, jnp.int32),
+            pltpu.VMEM((rows, width), F32),
+            pltpu.VMEM((rows, width), BF16),
+            pltpu.VMEM((width, width), BF16),
             pltpu.VMEM((width, width), F32),
             pltpu.VMEM((width, width), F32),
             pltpu.VMEM((width, width), BF16),
@@ -310,22 +307,10 @@
             collective_id=0, has_side_effects=True, vmem_limit_bytes=VMEM_LIMIT
         ),
         cost_estimate=pl.CostEstimate(
-            flops=3 * flops, bytes_accessed=4 * rows * width, transcendentals=0
+            flops=4 * flops, bytes_accessed=4 * rows * width, transcendentals=0
         ),
     )(three_index, virtual_energy.reshape(VT, TS), occupied_energy, tile_occupied, tile_virtual,
       tile_exponent)
-    steps = 4
-    return pl.pallas_call(
-        finish,
-        grid=(steps,),
-        out_shape=jax.ShapeDtypeStruct((rows, width), BF16),
-        in_specs=[vmem] * 3,
-        out_specs=pl.BlockSpec((rows // steps, width), lambda i: (i, 0)),
-        compiler_params=pltpu.CompilerParams(vmem_limit_bytes=8 * 1024 * 1024),
-        cost_estimate=pl.CostEstimate(
-            flops=flops, bytes_accessed=2 * rows * width, transcendentals=0
-        ),
-    )(total, other, off_amp)
 
 
 def solution(mesh):

time: 25.7 us -> 27.6 us (1.074)
  Pallas kernels: 25.6 us -> 26.7 us
  local copies, waits for them, and re-layouts: 0 us -> 0.77 us
    pallas_call x2 -> x1, Pallas kernels: 25.6 us -> 26.7 us  [pair_body(): pl.pallas_call(functools.partial(kernel, W, Z), out_shape=pltpu.VMEM((row...]
    unnamed x0 -> x1, local copies, waits for them, and re-layouts: none -> 0.77 us
where the time goes in v4:
time: 27.6 us; the launch traced here: 27.4 us
  Pallas kernels  26.7 us (97%)
  local copies, waits for them, and re-layouts  0.77 us (3%)
    pallas_call x1, Pallas kernels, pair_body(): pl.pallas_call(functools.partial(kernel, W, Z), out_shape=pltpu.VMEM((row...  26.7 us
    unnamed x1, local copies, waits for them, and re-layouts  0.77 us

profile of v4, /device:TPU:0, one launch (start us, length us, event | category | flops | bytes accessed | tf_op | source)
XLA Modules:
  0.0 27.4 jit_solution(10461245222586241928)
XLA Ops:
  0.0 26.7 %shard_map.64 = bf16[896,256]{1,0:T(8,128)(2,1)S(1)} custom-call(bf16[896,256]{1,0:T(8,128)(2,1)} %b_hbm.1, f32[157,128]{1,0:T(8,128)} %bitcast.1, f32[64]{0:T(128)} %occ_hbm.1, s32[4]{0:T(128)} %to_hbm.1, s32[4]{0:T(128)} %tv_hbm.1, s32[4]{0:T(128)} %te_hbm.1), custom_call_target="tpu_custom_call" | custom-call | flops 469762048 | bytes 917504 | tf_op jit(solution)/shard_map/pallas_call | solution.py:274
  26.7 0.8 %copy.8 = bf16[896,256]{1,0:T(8,128)(2,1)} copy(bf16[896,256]{1,0:T(8,128)(2,1)S(1)} %shard_map.64) | data formatting | bytes 917504

commit v5 on v4

--- a/solution.py
+++ b/solution.py
@@ -68,7 +68,7 @@
 
 
 def kernel(
-    W, Z, b_hbm, ve_hbm, occ_hbm, to_hbm, tv_hbm, te_hbm, out_ref,
+    W, Z, parts, b_hbm, ve_hbm, occ_hbm, to_hbm, tv_hbm, te_hbm, out_ref,
     b_ref, ve_ref, occ_ref, to_ref, tv_ref, te_ref, own_product, other, off_amp,
     own_sum, off_sum, own_part, off_part, own_got, off_got, own_line, off_line,
     own_line_got, off_line_got, own_amp, stage, energy,
@@ -116,17 +116,26 @@
 
     here = pl.multiple_of((1 - j) * half, half)
     away = pl.multiple_of(j * half, half)
-    half_rows = [(away, here), (here, away)]
     own_at = pl.multiple_of(w * own_piece, own_piece)
     off_at = pl.multiple_of(s * off_piece, off_piece)
 
-    def send_b(k):
-        at = pl.ds(half_rows[k][0], half)
-        return remote(b_hbm.at[at], other.at[at], b_s.at[k], b_r.at[k], across)
-
-    def got_b(k):
-        at = pl.ds(half_rows[k][1], half)
-        return remote(b_hbm.at[at], other.at[at], b_s.at[k], b_r.at[k], across)
+    halves = [(away, here, parts[0]), (here, away, parts[1])]
+
+    def b_copy(src, dst, k, p):
+        sem = (len(parts[0]) if k else 0) + p
+        return remote(b_hbm.at[src], other.at[dst], b_s.at[sem], b_r.at[sem], across)
+
+    def b_rows(first, k, p):
+        start, count = parts[k][p]
+        return pl.ds(pl.multiple_of(first + start, 16), count)
+
+    def send_b(k, p):
+        at = b_rows(halves[k][0], k, p)
+        return b_copy(at, at, k, p)
+
+    def got_b(k, p):
+        at = b_rows(halves[k][1], k, p)
+        return b_copy(at, at, k, p)
 
     def group(k, ref):
         return remote(ref, ref, sems.at[2 * k], sems.at[2 * k + 1], across)
@@ -142,7 +151,8 @@
         return jnp.sum(jnp.where(pick, row, 0.0), axis=1, keepdims=True)
 
     pl.semaphore_wait(barrier, S - 1 + Z - 1)
-    send_b(0).start()
+    for p in range(len(parts[0])):
+        send_b(0, p).start()
 
     loads[0].wait()
     own_sum[...] = tn_dot(b_ref[...], b_ref[...])
@@ -169,24 +179,38 @@
     for k in line:
         remote(own_line, own_line_got.at[z], sems.at[2], sems.at[3], dev(k, s)).start()
 
-    here_rows = pl.ds(here, half)
-    away_rows = pl.ds(away, half)
-    send_b(0).wait_send()
-    send_b(1).start()
-    got_b(0).wait_recv()
-
-    @pl.when(j == 0)
-    def _():
-        off_sum[...] = tn_dot(b_ref[here_rows, :], other[here_rows, :])
-
-    @pl.when(j == 1)
-    def _():
-        off_sum[...] = tn_dot(other[here_rows, :], b_ref[here_rows, :])
+    for p in range(len(parts[0])):
+        if p == len(parts[0]) - 1:
+            for sent in range(len(parts[0])):
+                send_b(0, sent).wait_send()
+            send_b(1, 0).start()
+        got_b(0, p).wait_recv()
+        at = b_rows(here, 0, p)
+
+        @pl.when(j == 0)
+        def _():
+            value = tn_dot(b_ref[at, :], other[at, :])
+            off_sum[...] = value if p == 0 else off_sum[...] + value
+
+        @pl.when(j == 1)
+        def _():
+            value = tn_dot(other[at, :], b_ref[at, :])
+            off_sum[...] = value if p == 0 else off_sum[...] + value
 
     off_part[...] = off_sum[...].astype(BF16)
     for k in plane:
         remote(off_part.at[pl.ds(pl.multiple_of(k * off_piece, off_piece), off_piece)],
                off_got.at[s], sems.at[6], sems.at[7], dev(z, k)).start()
+
+    off_scattered = group(3, off_got.at[pl.ds(0, S - 1)])
+    off_scattered.wait_recv()
+    send_b(1, 1).start()
+    off_total = off_sum[pl.ds(off_at, off_piece), :]
+    for k in range(S):
+        off_total = off_total + off_got[k].astype(F32)
+    off_line[...] = off_total.astype(BF16)
+    for k in line:
+        remote(off_line, off_line_got.at[z], sems.at[8], sems.at[9], dev(k, s)).start()
 
     own_lined = group(1, own_line_got.at[pl.ds(0, Z - 1)])
     own_lined.wait_recv()
@@ -206,19 +230,6 @@
     for k in side:
         remote(own_amp.at[own_rows], own_amp.at[own_rows],
                sems.at[4], sems.at[5], dev(z, j * W + k)).start()
-
-    off_scattered = group(3, off_got.at[pl.ds(0, S - 1)])
-    off_scattered.wait_recv()
-    off_total = off_sum[pl.ds(off_at, off_piece), :]
-    for k in range(S):
-        off_total = off_total + off_got[k].astype(F32)
-    off_line[...] = off_total.astype(BF16)
-    for k in line:
-        remote(off_line, off_line_got.at[z], sems.at[8], sems.at[9], dev(k, s)).start()
-
-    own_gathered = group(2, own_amp.at[pl.ds(0, (W - 1) * own_piece)])
-    own_gathered.wait_recv()
-    own_product[...] = nn_dot(b_ref[...], own_amp[...])
     own_scattered.wait_send()
     own_lined.wait_send()
     off_scattered.wait_send()
@@ -240,18 +251,21 @@
     for k in plane:
         remote(stage.at[lax.div(k, W)], off_amp.at[off_rows],
                sems.at[10], sems.at[11], dev(z, k)).start()
+    send_b(1, 2).start()
     off_amp[off_rows, :] = stage[j]
+
+    own_gathered = group(2, own_amp.at[pl.ds(0, (W - 1) * own_piece)])
+    own_gathered.wait_recv()
+    own_product[...] = nn_dot(b_ref[...], own_amp[...])
     own_gathered.wait_send()
     off_lined.wait_send()
     off_gathered = group(5, off_amp.at[pl.ds(0, (S - 1) * off_piece)])
     off_gathered.wait_send()
+    send_b(1, 0).wait_send()
+    send_b(1, 1).wait_send()
     off_gathered.wait_recv()
 
-    for at, later in ((here_rows, False), (away_rows, True)):
-        if later:
-            send_b(1).wait_send()
-            got_b(1).wait_recv()
-
+    def result(at):
         @pl.when(j == 0)
         def _():
             out_ref[at, :] = (own_product[at, :] + nt_dot(other[at, :], off_amp[...])).astype(BF16)
@@ -259,6 +273,16 @@
         @pl.when(j == 1)
         def _():
             out_ref[at, :] = (own_product[at, :] + nn_dot(other[at, :], off_amp[...])).astype(BF16)
+
+    result(pl.ds(here, half))
+    for p in range(3):
+        got_b(1, p).wait_recv()
+        if p > 0:
+            start, count = parts[1][p]
+            if p == 1:
+                start, count = 0, parts[1][0][1] + count
+            result(pl.ds(pl.multiple_of(away + start, 16), count))
+    send_b(1, 2).wait_send()
 
 
 def pair_body(W, Z, three_index, occupied_energy, virtual_energy, tile_occupied, tile_virtual,
@@ -267,12 +291,19 @@
     S = 2 * W
     own_piece = width // W
     off_piece = width // S
+    half = rows // 2
+    first = half // 32 * 16
+    small = half // 112 * 16
+    parts = (
+        ((0, first), (first, half - first)),
+        ((0, small), (small, first), (small + first, half - first - small)),
+    )
     hbm = pl.BlockSpec(memory_space=pltpu.HBM)
     vmem = pl.BlockSpec(memory_space=pltpu.VMEM)
     dma = pltpu.SemaphoreType.DMA
     flops = 2 * rows * width * width
     return pl.pallas_call(
-        functools.partial(kernel, W, Z),
+        functools.partial(kernel, W, Z, parts),
         out_shape=pltpu.VMEM((rows, width), BF16),
         in_specs=[hbm] * 6,
         out_specs=vmem,
@@ -300,7 +331,7 @@
             pltpu.VMEM((2, off_piece, width), BF16),
             pltpu.VMEM((8, TS), F32),
             dma((6,)),
-            dma((2,)), dma((2,)),
+            dma((5,)), dma((5,)),
             dma((12,)),
         ],
         compiler_params=pltpu.CompilerParams(
@@ -319,7 +350,7 @@
     Z = mesh.shape["aux"] // W
 
     def body(*args):
-        if mesh.shape["pair"] == 2 and Z * W == 16 and args[0].shape[1] == 2 * TS:
+        if mesh.shape["pair"] == 2 and Z * W == 16 and args[0].shape[1] == 2 * TS and args[0].shape[0] % 224 == 0:
             return pair_body(W, Z, *args)
         return general_body(*args)
 

time: 27.6 us -> 25.4 us (0.920)
  Pallas kernels: 26.7 us -> 24.5 us
    pallas_call x1, Pallas kernels: 26.7 us -> 24.5 us  [pair_body(): pl.pallas_call(functools.partial(kernel, W, Z, parts), out_shape=pltpu.VM...]
where the time goes in v5:
time: 25.4 us; the launch traced here: 25.3 us
  Pallas kernels  24.5 us (96%)
  local copies, waits for them, and re-layouts  0.77 us (3%)
    pallas_call x1, Pallas kernels, pair_body(): pl.pallas_call(functools.partial(kernel, W, Z, parts), out_shape=pltpu.VM...  24.5 us
    unnamed x1, local copies, waits for them, and re-layouts  0.77 us

profile of v5, /device:TPU:0, one launch (start us, length us, event | category | flops | bytes accessed | tf_op | source)
XLA Modules:
  0.0 25.3 jit_solution(1840986516576455659)
XLA Ops:
  0.0 24.5 %shard_map.64 = bf16[896,256]{1,0:T(8,128)(2,1)S(1)} custom-call(bf16[896,256]{1,0:T(8,128)(2,1)} %b_hbm.1, f32[157,128]{1,0:T(8,128)} %bitcast.1, f32[64]{0:T(128)} %occ_hbm.1, s32[4]{0:T(128)} %to_hbm.1, s32[4]{0:T(128)} %tv_hbm.1, s32[4]{0:T(128)} %te_hbm.1), custom_call_target="tpu_custom_call" | custom-call | flops 469762048 | bytes 917504 | tf_op jit(solution)/shard_map/pallas_call | solution.py:305
  24.5 0.8 %copy.8 = bf16[896,256]{1,0:T(8,128)(2,1)} copy(bf16[896,256]{1,0:T(8,128)(2,1)S(1)} %shard_map.64) | data formatting | bytes 917504

commit v6 on v5

--- a/solution.py
+++ b/solution.py
@@ -70,13 +70,14 @@
 def kernel(
     W, Z, parts, b_hbm, ve_hbm, occ_hbm, to_hbm, tv_hbm, te_hbm, out_ref,
     b_ref, ve_ref, occ_ref, to_ref, tv_ref, te_ref, own_product, other, off_amp,
-    own_sum, off_sum, own_part, off_part, own_got, off_got, own_line, off_line,
+    own_sum, off_send, off_core, off_sum, own_part, off_part, own_got, off_got, own_line, off_line,
     own_line_got, off_line_got, own_amp, stage, energy,
-    load, b_s, b_r, sems,
+    load, b_s, b_r, core_s, core_r, sems,
 ):
     rows, width = b_ref.shape
     half = rows // 2
     S = 2 * W
+    U = W
     own_piece = width // W
     off_piece = width // S
     aux = lax.axis_index("aux")
@@ -84,6 +85,8 @@
     z = lax.div(aux, W)
     w = lax.rem(aux, W)
     s = j * W + w
+    core = lax.rem(w, 2)
+    u = lax.div(s, 2)
 
     def dev(line, place):
         return {"aux": line * W + lax.rem(place, W), "pair": lax.div(place, W)}
@@ -95,7 +98,8 @@
         )
 
     across = dev(z, lax.rem(s + W, S))
-    plane = [lax.rem(s + i, S) for i in range(1, S)]
+    sibling = dev(z, 2 * u + 1 - core)
+    equal = [lax.rem(u + i, U) for i in range(1, U)]
     side = [lax.rem(w + i, W) for i in range(1, W)]
     line = [lax.rem(z + i, Z) for i in range(1, Z)]
 
@@ -107,8 +111,10 @@
         ])
     ]
     barrier = pltpu.get_barrier_semaphore()
-    for k in plane:
-        pl.semaphore_signal(barrier, inc=1, device_id=dev(z, k), device_id_type=MESH)
+    greeted = [dev(z, j * W + k) for k in side]
+    greeted += [dev(z, lax.rem((1 - j) * W + 2 * i + core, S)) for i in range(W // 2)]
+    for target in greeted:
+        pl.semaphore_signal(barrier, inc=1, device_id=target, device_id_type=MESH)
     for k in line:
         pl.semaphore_signal(barrier, inc=1, device_id=dev(k, s), device_id_type=MESH)
     for one in loads:
@@ -117,7 +123,10 @@
     here = pl.multiple_of((1 - j) * half, half)
     away = pl.multiple_of(j * half, half)
     own_at = pl.multiple_of(w * own_piece, own_piece)
-    off_at = pl.multiple_of(s * off_piece, off_piece)
+    mine = pl.multiple_of(core * TS, TS)
+    theirs = pl.multiple_of((1 - core) * TS, TS)
+    off_at = pl.multiple_of(u * off_piece, off_piece)
+    off_rows = pl.ds(pl.multiple_of(core * TS + u * off_piece, off_piece), off_piece)
 
     halves = [(away, here, parts[0]), (here, away, parts[1])]
 
@@ -150,7 +159,7 @@
             lax.broadcasted_iota(jnp.int32, shape, 0) + first)
         return jnp.sum(jnp.where(pick, row, 0.0), axis=1, keepdims=True)
 
-    pl.semaphore_wait(barrier, S - 1 + Z - 1)
+    pl.semaphore_wait(barrier, len(greeted) + Z - 1)
     for p in range(len(parts[0])):
         send_b(0, p).start()
 
@@ -166,7 +175,7 @@
     for t in range(4):
         energy[t:t + 1, :] = ve_ref[pl.ds(tv_ref[t], 1), :] - occ_ref[to_ref[t]]
     own_got[w] = jnp.zeros(own_got.shape[1:], BF16)
-    off_got[s] = jnp.zeros(off_got.shape[1:], BF16)
+    off_got[u] = jnp.zeros(off_got.shape[1:], BF16)
     own_line_got[z] = jnp.zeros(own_line_got.shape[1:], BF16)
     off_line_got[z] = jnp.zeros(off_line_got.shape[1:], BF16)
 
@@ -179,6 +188,7 @@
     for k in line:
         remote(own_line, own_line_got.at[z], sems.at[2], sems.at[3], dev(k, s)).start()
 
+    off_core_copy = remote(off_send, off_core, core_s.at[0], core_r.at[0], sibling)
     for p in range(len(parts[0])):
         if p == len(parts[0]) - 1:
             for sent in range(len(parts[0])):
@@ -187,26 +197,35 @@
         got_b(0, p).wait_recv()
         at = b_rows(here, 0, p)
 
-        @pl.when(j == 0)
-        def _():
-            value = tn_dot(b_ref[at, :], other[at, :])
-            off_sum[...] = value if p == 0 else off_sum[...] + value
-
-        @pl.when(j == 1)
-        def _():
-            value = tn_dot(other[at, :], b_ref[at, :])
-            off_sum[...] = value if p == 0 else off_sum[...] + value
-
+        def product(target, cols):
+            @pl.when(j == 0)
+            def _():
+                value = tn_dot(b_ref[at, pl.ds(cols, TS)], other[at, :])
+                target[...] = value if p == 0 else target[...] + value
+
+            @pl.when(j == 1)
+            def _():
+                value = tn_dot(other[at, pl.ds(cols, TS)], b_ref[at, :])
+                target[...] = value if p == 0 else target[...] + value
+
+        product(off_send, theirs)
+        if p == len(parts[0]) - 1:
+            off_core_copy.start()
+        product(off_sum, mine)
+
+    off_core_copy.wait_recv()
+    off_sum[...] += off_core[...]
     off_part[...] = off_sum[...].astype(BF16)
-    for k in plane:
+    for k in equal:
         remote(off_part.at[pl.ds(pl.multiple_of(k * off_piece, off_piece), off_piece)],
-               off_got.at[s], sems.at[6], sems.at[7], dev(z, k)).start()
-
-    off_scattered = group(3, off_got.at[pl.ds(0, S - 1)])
+               off_got.at[u], sems.at[6], sems.at[7], dev(z, 2 * k + core)).start()
+
+    off_scattered = group(3, off_got.at[pl.ds(0, U - 1)])
+    off_scattered.wait_send()
+    send_b(1, 1).start()
     off_scattered.wait_recv()
-    send_b(1, 1).start()
     off_total = off_sum[pl.ds(off_at, off_piece), :]
-    for k in range(S):
+    for k in range(U):
         off_total = off_total + off_got[k].astype(F32)
     off_line[...] = off_total.astype(BF16)
     for k in line:
@@ -232,10 +251,10 @@
                sems.at[4], sems.at[5], dev(z, j * W + k)).start()
     own_scattered.wait_send()
     own_lined.wait_send()
-    off_scattered.wait_send()
-
-    row_e = down(energy[pl.ds(j, 1), :], w * off_piece, off_piece)
-    row_s = scale(j)
+    off_core_copy.wait_send()
+
+    row_e = down(energy[pl.ds(core, 1), :], u * off_piece, off_piece)
+    row_s = scale(core)
     off_lined = group(4, off_line_got.at[pl.ds(0, Z - 1)])
     off_lined.wait_recv()
     for k in range(Z):
@@ -247,23 +266,29 @@
         value = off_total[:, cols]
         stage[0, :, cols] = (value * (col_s * col_s) * row_s / denominator).astype(BF16)
         stage[1, :, cols] = (value * (row_s * row_s) * col_s / denominator).astype(BF16)
-    off_rows = pl.ds(off_at, off_piece)
-    for k in plane:
-        remote(stage.at[lax.div(k, W)], off_amp.at[off_rows],
-               sems.at[10], sems.at[11], dev(z, k)).start()
+    for k in equal:
+        remote(stage.at[lax.div(k, U // 2)], off_amp.at[off_rows],
+               sems.at[10], sems.at[11], dev(z, 2 * k + core)).start()
+    off_amp[off_rows, :] = stage[j]
+    off_gathered = group(5, off_amp.at[pl.ds(0, (U - 1) * off_piece)])
+    off_gathered.wait_send()
     send_b(1, 2).start()
-    off_amp[off_rows, :] = stage[j]
 
     own_gathered = group(2, own_amp.at[pl.ds(0, (W - 1) * own_piece)])
     own_gathered.wait_recv()
     own_product[...] = nn_dot(b_ref[...], own_amp[...])
+    off_gathered.wait_recv()
+
+    def forward(first):
+        place = off_amp.at[pl.ds(first, TS)]
+        return remote(place, place, core_s.at[1], core_r.at[1], sibling)
+
+    forward(mine).start()
     own_gathered.wait_send()
     off_lined.wait_send()
-    off_gathered = group(5, off_amp.at[pl.ds(0, (S - 1) * off_piece)])
-    off_gathered.wait_send()
     send_b(1, 0).wait_send()
     send_b(1, 1).wait_send()
-    off_gathered.wait_recv()
+    forward(theirs).wait_recv()
 
     def result(at):
         @pl.when(j == 0)
@@ -283,6 +308,7 @@
                 start, count = 0, parts[1][0][1] + count
             result(pl.ds(pl.multiple_of(away + start, 16), count))
     send_b(1, 2).wait_send()
+    forward(mine).wait_send()
 
 
 def pair_body(W, Z, three_index, occupied_energy, virtual_energy, tile_occupied, tile_virtual,
@@ -293,10 +319,11 @@
     off_piece = width // S
     half = rows // 2
     first = half // 32 * 16
-    small = half // 112 * 16
+    small = 2 * half // 112 * 16
+    middle = half // 32 * 16 - 16
     parts = (
         ((0, first), (first, half - first)),
-        ((0, small), (small, first), (small + first, half - first - small)),
+        ((0, small), (small, middle), (small + middle, half - middle - small)),
     )
     hbm = pl.BlockSpec(memory_space=pltpu.HBM)
     vmem = pl.BlockSpec(memory_space=pltpu.VMEM)
@@ -318,11 +345,13 @@
             pltpu.VMEM((rows, width), BF16),
             pltpu.VMEM((width, width), BF16),
             pltpu.VMEM((width, width), F32),
-            pltpu.VMEM((width, width), F32),
+            pltpu.VMEM((TS, width), F32),
+            pltpu.VMEM((TS, width), F32),
+            pltpu.VMEM((TS, width), F32),
             pltpu.VMEM((width, width), BF16),
-            pltpu.VMEM((width, width), BF16),
+            pltpu.VMEM((TS, width), BF16),
             pltpu.VMEM((W, own_piece, width), BF16),
-            pltpu.VMEM((S, off_piece, width), BF16),
+            pltpu.VMEM((W, off_piece, width), BF16),
             pltpu.VMEM((own_piece, width), BF16),
             pltpu.VMEM((off_piece, width), BF16),
             pltpu.VMEM((Z, own_piece, width), BF16),
@@ -332,6 +361,7 @@
             pltpu.VMEM((8, TS), F32),
             dma((6,)),
             dma((5,)), dma((5,)),
+            dma((2,)), dma((2,)),
             dma((12,)),
         ],
         compiler_params=pltpu.CompilerParams(

time: 25.4 us -> 26.2 us (1.031)
  Pallas kernels: 24.5 us -> 25.3 us
    pallas_call x1, Pallas kernels: 24.5 us -> 25.3 us  [pair_body(): pl.pallas_call(functools.partial(kernel, W, Z, parts), out_shape=pltpu.VM...]
where the time goes in v6:
time: 26.2 us; the launch traced here: 26.1 us
  Pallas kernels  25.3 us (97%)
  local copies, waits for them, and re-layouts  0.77 us (3%)
    pallas_call x1, Pallas kernels, pair_body(): pl.pallas_call(functools.partial(kernel, W, Z, parts), out_shape=pltpu.VM...  25.3 us
    unnamed x1, local copies, waits for them, and re-layouts  0.77 us

profile of v6, /device:TPU:0, one launch (start us, length us, event | category | flops | bytes accessed | tf_op | source)
XLA Modules:
  0.0 26.1 jit_solution(11247970875632729571)
XLA Ops:
  0.0 25.3 %shard_map.64 = bf16[896,256]{1,0:T(8,128)(2,1)S(1)} custom-call(bf16[896,256]{1,0:T(8,128)(2,1)} %b_hbm.1, f32[157,128]{1,0:T(8,128)} %bitcast.1, f32[64]{0:T(128)} %occ_hbm.1, s32[4]{0:T(128)} %to_hbm.1, s32[4]{0:T(128)} %tv_hbm.1, s32[4]{0:T(128)} %te_hbm.1), custom_call_target="tpu_custom_call" | custom-call | flops 469762048 | bytes 917504 | tf_op jit(solution)/shard_map/pallas_call | solution.py:332
  25.3 0.8 %copy.8 = bf16[896,256]{1,0:T(8,128)(2,1)} copy(bf16[896,256]{1,0:T(8,128)(2,1)S(1)} %shard_map.64) | data formatting | bytes 917504

commit v7 on v5

--- a/solution.py
+++ b/solution.py
@@ -123,7 +123,7 @@
 
     def b_copy(src, dst, k, p):
         sem = (len(parts[0]) if k else 0) + p
-        return remote(b_hbm.at[src], other.at[dst], b_s.at[sem], b_r.at[sem], across)
+        return remote(b_ref.at[src], other.at[dst], b_s.at[sem], b_r.at[sem], across)
 
     def b_rows(first, k, p):
         start, count = parts[k][p]
@@ -151,10 +151,10 @@
         return jnp.sum(jnp.where(pick, row, 0.0), axis=1, keepdims=True)
 
     pl.semaphore_wait(barrier, S - 1 + Z - 1)
+    loads[0].wait()
     for p in range(len(parts[0])):
         send_b(0, p).start()
 
-    loads[0].wait()
     own_sum[...] = tn_dot(b_ref[...], b_ref[...])
     own_part[...] = own_sum[...].astype(BF16)
     for k in side:
@@ -179,13 +179,14 @@
     for k in line:
         remote(own_line, own_line_got.at[z], sems.at[2], sems.at[3], dev(k, s)).start()
 
-    for p in range(len(parts[0])):
-        if p == len(parts[0]) - 1:
+    for p in range(0, len(parts[0]), 2):
+        if p == len(parts[0]) - 2:
             for sent in range(len(parts[0])):
                 send_b(0, sent).wait_send()
             send_b(1, 0).start()
         got_b(0, p).wait_recv()
-        at = b_rows(here, 0, p)
+        got_b(0, p + 1).wait_recv()
+        at = pl.ds(pl.multiple_of(here + parts[0][p][0], 16), parts[0][p][1] + parts[0][p + 1][1])
 
         @pl.when(j == 0)
         def _():
@@ -295,7 +296,7 @@
     first = half // 32 * 16
     small = half // 112 * 16
     parts = (
-        ((0, first), (first, half - first)),
+        tuple((i * first // 2, first // 2) for i in range(4)),
         ((0, small), (small, first), (small + first, half - first - small)),
     )
     hbm = pl.BlockSpec(memory_space=pltpu.HBM)
@@ -331,7 +332,7 @@
             pltpu.VMEM((2, off_piece, width), BF16),
             pltpu.VMEM((8, TS), F32),
             dma((6,)),
-            dma((5,)), dma((5,)),
+            dma((7,)), dma((7,)),
             dma((12,)),
         ],
         compiler_params=pltpu.CompilerParams(

time: 25.4 us -> 25.2 us (level)
  Pallas kernels: 24.5 us -> 24.2 us
    pallas_call x1, Pallas kernels: 24.5 us -> 24.2 us  [pair_body(): pl.pallas_call(functools.partial(kernel, W, Z, parts), out_shape=pltpu.VM...]
where the time goes in v7:
time: 25.2 us; the launch traced here: 25 us
  Pallas kernels  24.2 us (96%)
  local copies, waits for them, and re-layouts  0.77 us (3%)
    pallas_call x1, Pallas kernels, pair_body(): pl.pallas_call(functools.partial(kernel, W, Z, parts), out_shape=pltpu.VM...  24.2 us
    unnamed x1, local copies, waits for them, and re-layouts  0.77 us

profile of v7, /device:TPU:0, one launch (start us, length us, event | category | flops | bytes accessed | tf_op | source)
XLA Modules:
  0.0 25.0 jit_solution(11821176825998853874)
XLA Ops:
  0.0 24.2 %shard_map.64 = bf16[896,256]{1,0:T(8,128)(2,1)S(1)} custom-call(bf16[896,256]{1,0:T(8,128)(2,1)} %b_hbm.1, f32[157,128]{1,0:T(8,128)} %bitcast.1, f32[64]{0:T(128)} %occ_hbm.1, s32[4]{0:T(128)} %to_hbm.1, s32[4]{0:T(128)} %tv_hbm.1, s32[4]{0:T(128)} %te_hbm.1), custom_call_target="tpu_custom_call" | custom-call | flops 469762048 | bytes 917504 | tf_op jit(solution)/shard_map/pallas_call | solution.py:306
  24.2 0.8 %copy.8 = bf16[896,256]{1,0:T(8,128)(2,1)} copy(bf16[896,256]{1,0:T(8,128)(2,1)S(1)} %shard_map.64) | data formatting | bytes 917504

commit v8 on v7

--- a/solution.py
+++ b/solution.py
@@ -95,7 +95,9 @@
         )
 
     across = dev(z, lax.rem(s + W, S))
-    plane = [lax.rem(s + i, S) for i in range(1, S)]
+    far = [(1 - j) * W + lax.rem(w + i, W) for i in range(W)]
+    near = [j * W + lax.rem(w + i, W) for i in range(1, W)]
+    plane = far + near
     side = [lax.rem(w + i, W) for i in range(1, W)]
     line = [lax.rem(z + i, Z) for i in range(1, Z)]
 
@@ -123,7 +125,8 @@
 
     def b_copy(src, dst, k, p):
         sem = (len(parts[0]) if k else 0) + p
-        return remote(b_ref.at[src], other.at[dst], b_s.at[sem], b_r.at[sem], across)
+        source = b_hbm if k == 0 and p == 0 else b_ref
+        return remote(source.at[src], other.at[dst], b_s.at[sem], b_r.at[sem], across)
 
     def b_rows(first, k, p):
         start, count = parts[k][p]
@@ -151,8 +154,9 @@
         return jnp.sum(jnp.where(pick, row, 0.0), axis=1, keepdims=True)
 
     pl.semaphore_wait(barrier, S - 1 + Z - 1)
+    send_b(0, 0).start()
     loads[0].wait()
-    for p in range(len(parts[0])):
+    for p in range(1, len(parts[0])):
         send_b(0, p).start()
 
     own_sum[...] = tn_dot(b_ref[...], b_ref[...])
@@ -188,20 +192,25 @@
         got_b(0, p + 1).wait_recv()
         at = pl.ds(pl.multiple_of(here + parts[0][p][0], 16), parts[0][p][1] + parts[0][p + 1][1])
 
-        @pl.when(j == 0)
-        def _():
-            value = tn_dot(b_ref[at, :], other[at, :])
-            off_sum[...] = value if p == 0 else off_sum[...] + value
-
-        @pl.when(j == 1)
-        def _():
-            value = tn_dot(other[at, :], b_ref[at, :])
-            off_sum[...] = value if p == 0 else off_sum[...] + value
-
-    off_part[...] = off_sum[...].astype(BF16)
-    for k in plane:
-        remote(off_part.at[pl.ds(pl.multiple_of(k * off_piece, off_piece), off_piece)],
-               off_got.at[s], sems.at[6], sems.at[7], dev(z, k)).start()
+        for side_chips, first in ((far, 1 - j), (near, j)):
+            cols = pl.ds(pl.multiple_of(first * TS, TS), TS)
+
+            @pl.when(j == 0)
+            def _():
+                value = tn_dot(b_ref[at, cols], other[at, :])
+                off_sum[cols, :] = value if p == 0 else off_sum[cols, :] + value
+
+            @pl.when(j == 1)
+            def _():
+                value = tn_dot(other[at, cols], b_ref[at, :])
+                off_sum[cols, :] = value if p == 0 else off_sum[cols, :] + value
+
+            if p == len(parts[0]) - 2:
+                off_part[cols, :] = off_sum[cols, :].astype(BF16)
+                for k in side_chips:
+                    piece = pl.ds(pl.multiple_of(k * off_piece, off_piece), off_piece)
+                    remote(off_part.at[piece], off_got.at[s], sems.at[6], sems.at[7],
+                           dev(z, k)).start()
 
     off_scattered = group(3, off_got.at[pl.ds(0, S - 1)])
     off_scattered.wait_recv()
@@ -294,10 +303,11 @@
     off_piece = width // S
     half = rows // 2
     first = half // 32 * 16
-    small = half // 112 * 16
+    small = 32
+    middle = 240
     parts = (
         tuple((i * first // 2, first // 2) for i in range(4)),
-        ((0, small), (small, first), (small + first, half - first - small)),
+        ((0, small), (small, middle), (small + middle, half - middle - small)),
     )
     hbm = pl.BlockSpec(memory_space=pltpu.HBM)
     vmem = pl.BlockSpec(memory_space=pltpu.VMEM)
@@ -351,7 +361,7 @@
     Z = mesh.shape["aux"] // W
 
     def body(*args):
-        if mesh.shape["pair"] == 2 and Z * W == 16 and args[0].shape[1] == 2 * TS and args[0].shape[0] % 224 == 0:
+        if mesh.shape["pair"] == 2 and Z * W == 16 and args[0].shape[1] == 2 * TS and args[0].shape[0] == 896:
             return pair_body(W, Z, *args)
         return general_body(*args)
 

time: 25.2 us -> 25.5 us (1.012)
  Pallas kernels: 24.2 us -> 24.6 us
    pallas_call x1, Pallas kernels: 24.2 us -> 24.6 us  [pair_body(): pl.pallas_call(functools.partial(kernel, W, Z, parts), out_shape=pltpu.VM...]
where the time goes in v8:
time: 25.5 us; the launch traced here: 25.4 us
  Pallas kernels  24.6 us (96%)
  local copies, waits for them, and re-layouts  0.77 us (3%)
    pallas_call x1, Pallas kernels, pair_body(): pl.pallas_call(functools.partial(kernel, W, Z, parts), out_shape=pltpu.VM...  24.6 us
    unnamed x1, local copies, waits for them, and re-layouts  0.77 us

profile of v8, /device:TPU:0, one launch (start us, length us, event | category | flops | bytes accessed | tf_op | source)
XLA Modules:
  0.0 25.4 jit_solution(11280651726693161576)
XLA Ops:
  0.0 24.6 %shard_map.64 = bf16[896,256]{1,0:T(8,128)(2,1)S(1)} custom-call(bf16[896,256]{1,0:T(8,128)(2,1)} %b_hbm.1, f32[157,128]{1,0:T(8,128)} %bitcast.1, f32[64]{0:T(128)} %occ_hbm.1, s32[4]{0:T(128)} %to_hbm.1, s32[4]{0:T(128)} %tv_hbm.1, s32[4]{0:T(128)} %te_hbm.1), custom_call_target="tpu_custom_call" | custom-call | flops 469762048 | bytes 917504 | tf_op jit(solution)/shard_map/pallas_call | solution.py:316
  24.6 0.8 %copy.8 = bf16[896,256]{1,0:T(8,128)(2,1)} copy(bf16[896,256]{1,0:T(8,128)(2,1)S(1)} %shard_map.64) | data formatting | bytes 917504

commit v9 on v7

--- a/solution.py
+++ b/solution.py
@@ -166,9 +166,10 @@
     for t in range(4):
         energy[t:t + 1, :] = ve_ref[pl.ds(tv_ref[t], 1), :] - occ_ref[to_ref[t]]
     own_got[w] = jnp.zeros(own_got.shape[1:], BF16)
-    off_got[s] = jnp.zeros(off_got.shape[1:], BF16)
+    for h in range(2):
+        off_got[h, s] = jnp.zeros(off_got.shape[2:], BF16)
+        off_line_got[h, z] = jnp.zeros(off_line_got.shape[2:], BF16)
     own_line_got[z] = jnp.zeros(own_line_got.shape[1:], BF16)
-    off_line_got[z] = jnp.zeros(off_line_got.shape[1:], BF16)
 
     own_scattered = group(0, own_got.at[pl.ds(0, W - 1)])
     own_scattered.wait_recv()
@@ -188,30 +189,39 @@
         got_b(0, p + 1).wait_recv()
         at = pl.ds(pl.multiple_of(here + parts[0][p][0], 16), parts[0][p][1] + parts[0][p + 1][1])
 
-        @pl.when(j == 0)
-        def _():
-            value = tn_dot(b_ref[at, :], other[at, :])
-            off_sum[...] = value if p == 0 else off_sum[...] + value
-
-        @pl.when(j == 1)
-        def _():
-            value = tn_dot(other[at, :], b_ref[at, :])
-            off_sum[...] = value if p == 0 else off_sum[...] + value
-
-    off_part[...] = off_sum[...].astype(BF16)
-    for k in plane:
-        remote(off_part.at[pl.ds(pl.multiple_of(k * off_piece, off_piece), off_piece)],
-               off_got.at[s], sems.at[6], sems.at[7], dev(z, k)).start()
-
-    off_scattered = group(3, off_got.at[pl.ds(0, S - 1)])
-    off_scattered.wait_recv()
+        for h in range(2):
+            cols = slice(h * TS, (h + 1) * TS)
+
+            @pl.when(j == 0)
+            def _():
+                value = tn_dot(b_ref[at, :], other[at, cols])
+                off_sum[h] = value if p == 0 else off_sum[h] + value
+
+            @pl.when(j == 1)
+            def _():
+                value = tn_dot(other[at, :], b_ref[at, cols])
+                off_sum[h] = value if p == 0 else off_sum[h] + value
+
+            if p == len(parts[0]) - 2:
+                off_part[h] = off_sum[h].astype(BF16)
+                for k in plane:
+                    piece = pl.ds(pl.multiple_of(k * off_piece, off_piece), off_piece)
+                    remote(off_part.at[h, piece], off_got.at[h, s],
+                           sems.at[6 + 2 * h], sems.at[7 + 2 * h], dev(z, k)).start()
+
+    off_scattered = [group(3 + h, off_got.at[h, pl.ds(0, S - 1)]) for h in range(2)]
+    off_total = []
+    for h in range(2):
+        off_scattered[h].wait_recv()
+        total = off_sum[h, pl.ds(off_at, off_piece), :]
+        for k in range(S):
+            total = total + off_got[h, k].astype(F32)
+        off_total.append(total)
+        off_line[h] = total.astype(BF16)
+        for k in line:
+            remote(off_line.at[h], off_line_got.at[h, z],
+                   sems.at[10 + 2 * h], sems.at[11 + 2 * h], dev(k, s)).start()
     send_b(1, 1).start()
-    off_total = off_sum[pl.ds(off_at, off_piece), :]
-    for k in range(S):
-        off_total = off_total + off_got[k].astype(F32)
-    off_line[...] = off_total.astype(BF16)
-    for k in line:
-        remote(off_line, off_line_got.at[z], sems.at[8], sems.at[9], dev(k, s)).start()
 
     own_lined = group(1, own_line_got.at[pl.ds(0, Z - 1)])
     own_lined.wait_recv()
@@ -233,47 +243,56 @@
                sems.at[4], sems.at[5], dev(z, j * W + k)).start()
     own_scattered.wait_send()
     own_lined.wait_send()
-    off_scattered.wait_send()
+    for h in range(2):
+        off_scattered[h].wait_send()
 
     row_e = down(energy[pl.ds(j, 1), :], w * off_piece, off_piece)
     row_s = scale(j)
-    off_lined = group(4, off_line_got.at[pl.ds(0, Z - 1)])
-    off_lined.wait_recv()
-    for k in range(Z):
-        off_total = off_total + off_line_got[k].astype(F32)
+    off_rows = pl.ds(off_at, off_piece)
+    off_lined = [group(5 + h, off_line_got.at[h, pl.ds(0, Z - 1)]) for h in range(2)]
     for h in range(2):
         cols = slice(h * TS, (h + 1) * TS)
+        off_lined[h].wait_recv()
+        value = off_total[h]
+        for k in range(Z):
+            value = value + off_line_got[h, k].astype(F32)
         denominator = row_e + energy[2 + h:3 + h, :]
         col_s = scale(2 + h)
-        value = off_total[:, cols]
-        stage[0, :, cols] = (value * (col_s * col_s) * row_s / denominator).astype(BF16)
-        stage[1, :, cols] = (value * (row_s * row_s) * col_s / denominator).astype(BF16)
-    off_rows = pl.ds(off_at, off_piece)
-    for k in plane:
-        remote(stage.at[lax.div(k, W)], off_amp.at[off_rows],
-               sems.at[10], sems.at[11], dev(z, k)).start()
+        stage[h, 0] = (value * (col_s * col_s) * row_s / denominator).astype(BF16)
+        stage[h, 1] = (value * (row_s * row_s) * col_s / denominator).astype(BF16)
+        for k in plane:
+            remote(stage.at[h, lax.div(k, W)], off_amp.at[h, off_rows],
+                   sems.at[14 + 2 * h], sems.at[15 + 2 * h], dev(z, k)).start()
+        off_amp[h, off_rows, :] = stage[h, j]
     send_b(1, 2).start()
-    off_amp[off_rows, :] = stage[j]
 
     own_gathered = group(2, own_amp.at[pl.ds(0, (W - 1) * own_piece)])
     own_gathered.wait_recv()
     own_product[...] = nn_dot(b_ref[...], own_amp[...])
     own_gathered.wait_send()
-    off_lined.wait_send()
-    off_gathered = group(5, off_amp.at[pl.ds(0, (S - 1) * off_piece)])
-    off_gathered.wait_send()
+    off_gathered = [
+        group(7 + h, off_amp.at[h, pl.ds(0, (S - 1) * off_piece)]) for h in range(2)
+    ]
+    for h in range(2):
+        off_lined[h].wait_send()
+        off_gathered[h].wait_send()
     send_b(1, 0).wait_send()
     send_b(1, 1).wait_send()
-    off_gathered.wait_recv()
+    for h in range(2):
+        off_gathered[h].wait_recv()
 
     def result(at):
         @pl.when(j == 0)
         def _():
-            out_ref[at, :] = (own_product[at, :] + nt_dot(other[at, :], off_amp[...])).astype(BF16)
+            out_ref[at, :] = (own_product[at, :] + nt_dot(other[at, :TS], off_amp[0])
+                              + nt_dot(other[at, TS:], off_amp[1])).astype(BF16)
 
         @pl.when(j == 1)
         def _():
-            out_ref[at, :] = (own_product[at, :] + nn_dot(other[at, :], off_amp[...])).astype(BF16)
+            for h in range(2):
+                cols = slice(h * TS, (h + 1) * TS)
+                out_ref[at, cols] = (
+                    own_product[at, cols] + nn_dot(other[at, :], off_amp[h])).astype(BF16)
 
     result(pl.ds(here, half))
     for p in range(3):
@@ -317,23 +336,23 @@
             pltpu.SMEM(tile_exponent.shape, jnp.int32),
             pltpu.VMEM((rows, width), F32),
             pltpu.VMEM((rows, width), BF16),
+            pltpu.VMEM((2, width, TS), BF16),
+            pltpu.VMEM((width, width), F32),
+            pltpu.VMEM((2, width, TS), F32),
             pltpu.VMEM((width, width), BF16),
-            pltpu.VMEM((width, width), F32),
-            pltpu.VMEM((width, width), F32),
+            pltpu.VMEM((2, width, TS), BF16),
+            pltpu.VMEM((W, own_piece, width), BF16),
+            pltpu.VMEM((2, S, off_piece, TS), BF16),
+            pltpu.VMEM((own_piece, width), BF16),
+            pltpu.VMEM((2, off_piece, TS), BF16),
+            pltpu.VMEM((Z, own_piece, width), BF16),
+            pltpu.VMEM((2, Z, off_piece, TS), BF16),
             pltpu.VMEM((width, width), BF16),
-            pltpu.VMEM((width, width), BF16),
-            pltpu.VMEM((W, own_piece, width), BF16),
-            pltpu.VMEM((S, off_piece, width), BF16),
-            pltpu.VMEM((own_piece, width), BF16),
-            pltpu.VMEM((off_piece, width), BF16),
-            pltpu.VMEM((Z, own_piece, width), BF16),
-            pltpu.VMEM((Z, off_piece, width), BF16),
-            pltpu.VMEM((width, width), BF16),
-            pltpu.VMEM((2, off_piece, width), BF16),
+            pltpu.VMEM((2, 2, off_piece, TS), BF16),
             pltpu.VMEM((8, TS), F32),
             dma((6,)),
             dma((7,)), dma((7,)),
-            dma((12,)),
+            dma((18,)),
         ],
         compiler_params=pltpu.CompilerParams(
             collective_id=0, has_side_effects=True, vmem_limit_bytes=VMEM_LIMIT

time: 25.2 us -> 25.5 us (1.012)
  Pallas kernels: 24.2 us -> 24.6 us
    pallas_call x1, Pallas kernels: 24.2 us -> 24.6 us  [pair_body(): pl.pallas_call(functools.partial(kernel, W, Z, parts), out_shape=pltpu.VM...]
where the time goes in v9:
time: 25.5 us; the launch traced here: 25.3 us
  Pallas kernels  24.6 us (96%)
  local copies, waits for them, and re-layouts  0.77 us (3%)
    pallas_call x1, Pallas kernels, pair_body(): pl.pallas_call(functools.partial(kernel, W, Z, parts), out_shape=pltpu.VM...  24.6 us
    unnamed x1, local copies, waits for them, and re-layouts  0.77 us

profile of v9, /device:TPU:0, one launch (start us, length us, event | category | flops | bytes accessed | tf_op | source)
XLA Modules:
  0.0 25.3 jit_solution(12541428345815579566)
XLA Ops:
  0.0 24.6 %shard_map.64 = bf16[896,256]{1,0:T(8,128)(2,1)S(1)} custom-call(bf16[896,256]{1,0:T(8,128)(2,1)} %b_hbm.1, f32[157,128]{1,0:T(8,128)} %bitcast.1, f32[64]{0:T(128)} %occ_hbm.1, s32[4]{0:T(128)} %to_hbm.1, s32[4]{0:T(128)} %tv_hbm.1, s32[4]{0:T(128)} %te_hbm.1), custom_call_target="tpu_custom_call" | custom-call | flops 469762048 | bytes 917504 | tf_op jit(solution)/shard_map/pallas_call | solution.py:325
  24.6 0.8 %copy.8 = bf16[896,256]{1,0:T(8,128)(2,1)} copy(bf16[896,256]{1,0:T(8,128)(2,1)S(1)} %shard_map.64) | data formatting | bytes 917504

commit v10 on v9

--- a/solution.py
+++ b/solution.py
@@ -84,6 +84,8 @@
     z = lax.div(aux, W)
     w = lax.rem(aux, W)
     s = j * W + w
+    core = lax.rem(w, 2)
+    u = lax.div(s, 2)
 
     def dev(line, place):
         return {"aux": line * W + lax.rem(place, W), "pair": lax.div(place, W)}
@@ -96,6 +98,8 @@
 
     across = dev(z, lax.rem(s + W, S))
     plane = [lax.rem(s + i, S) for i in range(1, S)]
+    sibling = dev(z, 2 * u + 1 - core)
+    equal = [lax.rem(u + i, W) for i in range(1, W)]
     side = [lax.rem(w + i, W) for i in range(1, W)]
     line = [lax.rem(z + i, Z) for i in range(1, Z)]
 
@@ -117,7 +121,12 @@
     here = pl.multiple_of((1 - j) * half, half)
     away = pl.multiple_of(j * half, half)
     own_at = pl.multiple_of(w * own_piece, own_piece)
-    off_at = pl.multiple_of(s * off_piece, off_piece)
+
+    def piece_rows(k):
+        return pl.ds(pl.multiple_of(lax.rem(k, 2) * TS + lax.div(k, 2) * off_piece, off_piece),
+                     off_piece)
+
+    off_rows = piece_rows(s)
 
     halves = [(away, here, parts[0]), (here, away, parts[1])]
 
@@ -205,15 +214,14 @@
             if p == len(parts[0]) - 2:
                 off_part[h] = off_sum[h].astype(BF16)
                 for k in plane:
-                    piece = pl.ds(pl.multiple_of(k * off_piece, off_piece), off_piece)
-                    remote(off_part.at[h, piece], off_got.at[h, s],
+                    remote(off_part.at[h, piece_rows(k)], off_got.at[h, s],
                            sems.at[6 + 2 * h], sems.at[7 + 2 * h], dev(z, k)).start()
 
     off_scattered = [group(3 + h, off_got.at[h, pl.ds(0, S - 1)]) for h in range(2)]
     off_total = []
     for h in range(2):
         off_scattered[h].wait_recv()
-        total = off_sum[h, pl.ds(off_at, off_piece), :]
+        total = off_sum[h, off_rows, :]
         for k in range(S):
             total = total + off_got[h, k].astype(F32)
         off_total.append(total)
@@ -246,9 +254,8 @@
     for h in range(2):
         off_scattered[h].wait_send()
 
-    row_e = down(energy[pl.ds(j, 1), :], w * off_piece, off_piece)
-    row_s = scale(j)
-    off_rows = pl.ds(off_at, off_piece)
+    row_e = down(energy[pl.ds(core, 1), :], u * off_piece, off_piece)
+    row_s = scale(core)
     off_lined = [group(5 + h, off_line_got.at[h, pl.ds(0, Z - 1)]) for h in range(2)]
     for h in range(2):
         cols = slice(h * TS, (h + 1) * TS)
@@ -260,9 +267,9 @@
         col_s = scale(2 + h)
         stage[h, 0] = (value * (col_s * col_s) * row_s / denominator).astype(BF16)
         stage[h, 1] = (value * (row_s * row_s) * col_s / denominator).astype(BF16)
-        for k in plane:
-            remote(stage.at[h, lax.div(k, W)], off_amp.at[h, off_rows],
-                   sems.at[14 + 2 * h], sems.at[15 + 2 * h], dev(z, k)).start()
+        for k in equal:
+            remote(stage.at[h, lax.div(k, W // 2)], off_amp.at[h, off_rows],
+                   sems.at[14 + 2 * h], sems.at[15 + 2 * h], dev(z, 2 * k + core)).start()
         off_amp[h, off_rows, :] = stage[h, j]
     send_b(1, 2).start()
 
@@ -271,15 +278,23 @@
     own_product[...] = nn_dot(b_ref[...], own_amp[...])
     own_gathered.wait_send()
     off_gathered = [
-        group(7 + h, off_amp.at[h, pl.ds(0, (S - 1) * off_piece)]) for h in range(2)
+        group(7 + h, off_amp.at[h, pl.ds(0, (W - 1) * off_piece)]) for h in range(2)
     ]
     for h in range(2):
         off_lined[h].wait_send()
         off_gathered[h].wait_send()
     send_b(1, 0).wait_send()
     send_b(1, 1).wait_send()
+
+    def forward(h, which):
+        place = off_amp.at[h, pl.ds(pl.multiple_of(which * TS, TS), TS)]
+        return remote(place, place, sems.at[18 + 2 * h], sems.at[19 + 2 * h], sibling)
+
     for h in range(2):
         off_gathered[h].wait_recv()
+        forward(h, core).start()
+    for h in range(2):
+        forward(h, 1 - core).wait_recv()
 
     def result(at):
         @pl.when(j == 0)
@@ -303,6 +318,8 @@
                 start, count = 0, parts[1][0][1] + count
             result(pl.ds(pl.multiple_of(away + start, 16), count))
     send_b(1, 2).wait_send()
+    for h in range(2):
+        forward(h, core).wait_send()
 
 
 def pair_body(W, Z, three_index, occupied_energy, virtual_energy, tile_occupied, tile_virtual,
@@ -352,7 +369,7 @@
             pltpu.VMEM((8, TS), F32),
             dma((6,)),
             dma((7,)), dma((7,)),
-            dma((18,)),
+            dma((22,)),
         ],
         compiler_params=pltpu.CompilerParams(
             collective_id=0, has_side_effects=True, vmem_limit_bytes=VMEM_LIMIT

time: 25.5 us -> 25.4 us (level)
  the two profiles are of different devices: /device:TPU:0 before, /device:TPU:1 now
where the time goes in v10:
time: 25.4 us; the launch traced here: 25.3 us
  Pallas kernels  24.5 us (96%)
  local copies, waits for them, and re-layouts  0.77 us (3%)
    pallas_call x1, Pallas kernels, pair_body(): pl.pallas_call(functools.partial(kernel, W, Z, parts), out_shape=pltpu.VM...  24.5 us
    unnamed x1, local copies, waits for them, and re-layouts  0.77 us

profile of v10, /device:TPU:1, one launch (start us, length us, event | category | flops | bytes accessed | tf_op | source)
XLA Modules:
  0.0 25.3 jit_solution(14384908565975804937)
XLA Ops:
  0.0 24.5 %shard_map.64 = bf16[896,256]{1,0:T(8,128)(2,1)S(1)} custom-call(bf16[896,256]{1,0:T(8,128)(2,1)} %b_hbm.1, f32[157,128]{1,0:T(8,128)} %bitcast.1, f32[64]{0:T(128)} %occ_hbm.1, s32[4]{0:T(128)} %to_hbm.1, s32[4]{0:T(128)} %tv_hbm.1, s32[4]{0:T(128)} %te_hbm.1), custom_call_target="tpu_custom_call" | custom-call | flops 469762048 | bytes 917504 | tf_op jit(solution)/shard_map/pallas_call | solution.py:342
  24.5 0.8 %copy.8 = bf16[896,256]{1,0:T(8,128)(2,1)} copy(bf16[896,256]{1,0:T(8,128)(2,1)S(1)} %shard_map.64) | data formatting | bytes 917504

commit v11 on v9

--- a/solution.py
+++ b/solution.py
@@ -210,6 +210,9 @@
                            sems.at[6 + 2 * h], sems.at[7 + 2 * h], dev(z, k)).start()
 
     off_scattered = [group(3 + h, off_got.at[h, pl.ds(0, S - 1)]) for h in range(2)]
+    for h in range(2):
+        off_scattered[h].wait_send()
+    send_b(1, 1).start()
     off_total = []
     for h in range(2):
         off_scattered[h].wait_recv()
@@ -221,7 +224,6 @@
         for k in line:
             remote(off_line.at[h], off_line_got.at[h, z],
                    sems.at[10 + 2 * h], sems.at[11 + 2 * h], dev(k, s)).start()
-    send_b(1, 1).start()
 
     own_lined = group(1, own_line_got.at[pl.ds(0, Z - 1)])
     own_lined.wait_recv()
@@ -243,8 +245,6 @@
                sems.at[4], sems.at[5], dev(z, j * W + k)).start()
     own_scattered.wait_send()
     own_lined.wait_send()
-    for h in range(2):
-        off_scattered[h].wait_send()
 
     row_e = down(energy[pl.ds(j, 1), :], w * off_piece, off_piece)
     row_s = scale(j)
@@ -314,9 +314,10 @@
     half = rows // 2
     first = half // 32 * 16
     small = half // 112 * 16
+    middle = half // 28 * 16 + 16
     parts = (
         tuple((i * first // 2, first // 2) for i in range(4)),
-        ((0, small), (small, first), (small + first, half - first - small)),
+        ((0, small), (small, middle), (small + middle, half - middle - small)),
     )
     hbm = pl.BlockSpec(memory_space=pltpu.HBM)
     vmem = pl.BlockSpec(memory_space=pltpu.VMEM)

time: 25.5 us -> 24.8 us (0.973)
  Pallas kernels: 24.6 us -> 23.9 us
    pallas_call x1, Pallas kernels: 24.6 us -> 23.9 us  [pair_body(): pl.pallas_call(functools.partial(kernel, W, Z, parts), out_shape=pltpu.VM...]
where the time goes in v11:
time: 24.8 us; the launch traced here: 24.7 us
  Pallas kernels  23.9 us (96%)
  local copies, waits for them, and re-layouts  0.77 us (3%)
    pallas_call x1, Pallas kernels, pair_body(): pl.pallas_call(functools.partial(kernel, W, Z, parts), out_shape=pltpu.VM...  23.9 us
    unnamed x1, local copies, waits for them, and re-layouts  0.77 us

profile of v11, /device:TPU:0, one launch (start us, length us, event | category | flops | bytes accessed | tf_op | source)
XLA Modules:
  0.0 24.7 jit_solution(1146388964106867884)
XLA Ops:
  0.0 23.9 %shard_map.64 = bf16[896,256]{1,0:T(8,128)(2,1)S(1)} custom-call(bf16[896,256]{1,0:T(8,128)(2,1)} %b_hbm.1, f32[157,128]{1,0:T(8,128)} %bitcast.1, f32[64]{0:T(128)} %occ_hbm.1, s32[4]{0:T(128)} %to_hbm.1, s32[4]{0:T(128)} %tv_hbm.1, s32[4]{0:T(128)} %te_hbm.1), custom_call_target="tpu_custom_call" | custom-call | flops 469762048 | bytes 917504 | tf_op jit(solution)/shard_map/pallas_call | solution.py:326
  23.9 0.8 %copy.8 = bf16[896,256]{1,0:T(8,128)(2,1)} copy(bf16[896,256]{1,0:T(8,128)(2,1)S(1)} %shard_map.64) | data formatting | bytes 917504

commit v12 on v11

--- a/solution.py
+++ b/solution.py
@@ -314,7 +314,7 @@
     half = rows // 2
     first = half // 32 * 16
     small = half // 112 * 16
-    middle = half // 28 * 16 + 16
+    middle = half // 28 * 16 + 80
     parts = (
         tuple((i * first // 2, first // 2) for i in range(4)),
         ((0, small), (small, middle), (small + middle, half - middle - small)),

time: 24.8 us -> 24.8 us (level)
  no operation moved by 1% of the time
where the time goes in v12:
time: 24.8 us; the launch traced here: 24.7 us
  Pallas kernels  23.9 us (96%)
  local copies, waits for them, and re-layouts  0.77 us (3%)
    pallas_call x1, Pallas kernels, pair_body(): pl.pallas_call(functools.partial(kernel, W, Z, parts), out_shape=pltpu.VM...  23.9 us
    unnamed x1, local copies, waits for them, and re-layouts  0.77 us

profile of v12, /device:TPU:0, one launch (start us, length us, event | category | flops | bytes accessed | tf_op | source)
XLA Modules:
  0.0 24.7 jit_solution(10875382070306106006)
XLA Ops:
  0.0 23.9 %shard_map.64 = bf16[896,256]{1,0:T(8,128)(2,1)S(1)} custom-call(bf16[896,256]{1,0:T(8,128)(2,1)} %b_hbm.1, f32[157,128]{1,0:T(8,128)} %bitcast.1, f32[64]{0:T(128)} %occ_hbm.1, s32[4]{0:T(128)} %to_hbm.1, s32[4]{0:T(128)} %tv_hbm.1, s32[4]{0:T(128)} %te_hbm.1), custom_call_target="tpu_custom_call" | custom-call | flops 469762048 | bytes 917504 | tf_op jit(solution)/shard_map/pallas_call | solution.py:326
  23.9 0.8 %copy.8 = bf16[896,256]{1,0:T(8,128)(2,1)} copy(bf16[896,256]{1,0:T(8,128)(2,1)S(1)} %shard_map.64) | data formatting | bytes 917504
